TPU v7x, 32 devices: a whole 2x2x4 slice. The times are simulated.
32 devices in a mesh: expert: 8 (over y, x, core), context: 4 (over z).
Axes of the slice: x: 2, y: 2, z: 4, core: 2. Of those that a mesh axis runs over, the one named last changes fastest.
Arguments:
- tokens: bfloat16 [8192, 768], P(('expert', 'context')), may hold values from -6 to 6
- gain_attn: float32 [768], replicated, may hold values from 0.5 to 1.5
- w_query: bfloat16 [768, 768], replicated, may hold values from -0.21875 to 0.21875
- w_key: bfloat16 [768, 768], replicated, may hold values from -0.21875 to 0.21875
- w_value: bfloat16 [768, 768], replicated, may hold values from -0.21875 to 0.21875
- w_proj: bfloat16 [768, 768], replicated, may hold values from -3 to 3
- bias_table: float32 [32, 12], replicated, may hold values from -4 to 4
- gain_moe: float32 [768], replicated, may hold values from 0.5 to 1.5
- w_router: bfloat16 [768, 8], replicated, may hold values from -0.15625 to 0.15625
- w_up: bfloat16 [8, 768, 3072], P('expert'), may hold values from -0.21875 to 0.21875
- w_down: bfloat16 [8, 3072, 768], P('expert'), may hold values from -0.109375 to 0.109375
- routes: int32 [8192, 2], P(('expert', 'context')), may hold values from 0 to 7, all different within a row; in each aligned block of 256 rows (0 to 255, 256 to 511, ...) at most 128 rows name the same one
- bucket_ids: int32 [1024], replicated, may hold values from 0 to 31, as said below
- cotangent: bfloat16 [8192, 768], P(('expert', 'context')), may hold values from -6 to 6
Outputs:
- output: bfloat16 [8192, 768], P(('expert', 'context'))
- grad_tokens: bfloat16 [8192, 768], P(('expert', 'context'))
- grad_gain_attn: float32 [768], replicated
- grad_query: float32 [768, 768], replicated
- grad_key: float32 [768, 768], replicated
- grad_value: float32 [768, 768], replicated
- grad_proj: float32 [768, 768], replicated
- grad_table: float32 [32, 12], replicated
- grad_gain_moe: float32 [768], replicated
- grad_router: float32 [768, 8], replicated
- grad_up: float32 [8, 768, 3072], P('expert', None, 'context')
- grad_down: float32 [8, 3072, 768], P('expert', 'context')
Inputs may be any that keep to these rules, and one draw needn't show every extreme that they name: `routes`: in each aligned block of 256 rows (the rows of one device) no expert is named by more than 128 rows, a bound that some block reaches; the 2 experts of a row differ. `bucket_ids`: entry d is the bucket of a key d positions before its query; the entries never fall, rise by at most one from one distance to the next, entry 0 is 0 and the last entry is 31.
All inputs are finite; a program needn't handle non-finite values.
Results may differ from a plain program's by a relative error of at most 0.02.
Values may be sent and summed in bfloat16 or wider, within the bound.
No kernel may reach another device: no remote copies, remote signals or barrier semaphores. Data moves between devices by JAX's collectives and lax.ppermute only.
A program may use at most 192 MiB of HBM per device.

v0:
```python
from functools import partial
import math

import jax
import jax.numpy as jnp
from jax import lax
from jax.sharding import PartitionSpec as P

HEADS = 12


EPSILON = 1e-06
HIGHEST = lax.Precision.HIGHEST
BLOCK = 512
MASKED = -1000000000.0


def normalize(value, gain):
    scale = lax.rsqrt(jnp.mean(value * value, axis=1, keepdims=True) + EPSILON)
    return (value * scale * gain, scale)


def normalize_back(grad, value, scale, gain):
    normal = value * scale
    inner = grad * gain
    gain_grad = jnp.sum(grad * normal, axis=0)
    value_grad = scale * (inner - normal * jnp.mean(inner * normal, axis=1, keepdims=True))
    return (value_grad, gain_grad)


def split_blocks(piece):
    count = piece.shape[0]
    size = math.gcd(count, BLOCK)
    return (piece.reshape(count // size, size, HEADS, piece.shape[1] // HEADS), size)


def bias_window(dist_table, lowest, query_count, key_count):
    heads = dist_table.shape[0]
    span = query_count + key_count
    padding = dist_table.shape[1] // 3
    window = lax.dynamic_slice_in_dim(dist_table, lowest + padding, span, 1)
    tiled = jnp.tile(window, (1, query_count + 1))[:, : query_count * (span + 1)]
    skewed = tiled.reshape(heads, query_count, span + 1)
    return skewed[:, :, :key_count][:, :, ::-1]


def score_block(query_block, key_block, query_start, key_start, dist_table):
    factor = query_block.shape[2] ** (-0.5)
    query_count = query_block.shape[0]
    key_count = key_block.shape[0]
    raw = (
        jnp.einsum("qhd,khd->hqk", query_block, key_block, preferred_element_type=jnp.float32)
        * factor
    )
    offset = query_start - key_start
    distance = (
        offset
        + jnp.arange(query_count, dtype=jnp.int32)[:, None]
        - jnp.arange(key_count, dtype=jnp.int32)[None, :]
    )
    bias = bias_window(dist_table, offset - (key_count - 1), query_count, key_count)
    return jnp.where(distance[None] >= 0, raw + bias, MASKED)


def diagonal_sums(grid):
    heads, count, size = grid.shape
    turned = jnp.pad(grid[:, :, ::-1], ((0, 0), (0, 0), (0, count)))
    flat = turned.reshape(heads, count * (size + count))[:, : count * (size + count - 1)]
    return jnp.sum(flat.reshape(heads, count, size + count - 1), axis=1)


def shards(
    tokens,
    gain_attn,
    w_query,
    w_key,
    w_value,
    w_proj,
    bias_table,
    gain_moe,
    w_router,
    w_up,
    w_down,
    routes,
    bucket_ids,
    cotangent,
):
    rows, width = tokens.shape
    head_size = width // HEADS
    scale_factor = head_size ** (-0.5)
    experts = w_router.shape[1]
    buckets = bias_table.shape[0]
    picks = routes.shape[1]
    capacity = 2 * rows * picks // experts
    length = rows * lax.axis_size("context")
    first_place = lax.axis_index("context") * rows
    bucket_match = (bucket_ids[:, None] == jnp.arange(buckets, dtype=jnp.int32)[None, :]).astype(
        jnp.float32
    )
    per_distance = jnp.transpose(jnp.dot(bucket_match, bias_table, precision=HIGHEST))
    dist_table = jnp.pad(per_distance, ((0, 0), (length, length)))
    source = tokens.astype(jnp.float32)
    attention_normal, attention_scale = normalize(source, gain_attn)
    normed = attention_normal.astype(jnp.bfloat16)
    query = jnp.dot(normed, w_query, preferred_element_type=jnp.float32).astype(jnp.bfloat16)
    keys = jnp.dot(normed, w_key, preferred_element_type=jnp.float32).astype(jnp.bfloat16)
    values = jnp.dot(normed, w_value, preferred_element_type=jnp.float32).astype(jnp.bfloat16)
    query_heads = query.reshape(rows, HEADS, head_size)
    start_state = (
        jnp.full((HEADS, rows), -1e30, jnp.float32),
        jnp.zeros((HEADS, rows), jnp.float32),
        jnp.zeros((HEADS, rows, head_size), jnp.float32),
    )
    state = start_state
    pieces = (
        lax.all_gather(keys, "context", axis=0, tiled=True),
        lax.all_gather(values, "context", axis=0, tiled=True),
    )
    key_blocks, size = split_blocks(pieces[0])
    value_blocks, size = split_blocks(pieces[1])
    offsets = size * jnp.arange(key_blocks.shape[0], dtype=jnp.int32)

    def forward_visit(carry, entry):
        peak, total, accum = carry
        key_block, value_block, start = entry
        scores = score_block(query_heads, key_block, first_place, start, dist_table)
        new_peak = jnp.maximum(peak, jnp.max(scores, axis=2))
        factor = jnp.exp(peak - new_peak)
        weights = jnp.exp(scores - new_peak[:, :, None])
        total = total * factor + jnp.sum(weights, axis=2)
        accum = accum * factor[:, :, None] + jnp.einsum(
            "hqk,khd->hqd",
            weights.astype(jnp.bfloat16),
            value_block,
            preferred_element_type=jnp.float32,
        )
        return ((new_peak, total, accum), None)

    state, unused = lax.scan(forward_visit, state, (key_blocks, value_blocks, offsets))
    peak, total, accum = state
    mixed_exact = accum / total[:, :, None]
    log_total = peak + jnp.log(total)
    mixed = jnp.transpose(mixed_exact, (1, 0, 2)).reshape(rows, width).astype(jnp.bfloat16)
    middle = source + jnp.dot(mixed, w_proj, preferred_element_type=jnp.float32)
    moe_normal, moe_scale = normalize(middle, gain_moe)
    routed = moe_normal.astype(jnp.bfloat16)
    logits = jnp.dot(routed, w_router, preferred_element_type=jnp.float32)
    gates = jax.nn.softmax(jnp.take_along_axis(logits, routes, axis=1), axis=1)
    flat_routes = routes.reshape(-1)
    member = (flat_routes[:, None] == jnp.arange(experts, dtype=jnp.int32)[None, :]).astype(
        jnp.int32
    )
    earlier = jnp.cumsum(member, axis=0) - member
    slot = jnp.sum(earlier * member, axis=1).reshape(rows, picks)
    target = routes * capacity + slot
    select = (
        target[:, :, None] == jnp.arange(experts * capacity, dtype=jnp.int32)[None, None, :]
    ).astype(jnp.bfloat16)
    dispatch_matrix = jnp.sum(select, axis=1)
    send = jnp.einsum(
        "rs,rd->sd", dispatch_matrix, routed, preferred_element_type=jnp.float32
    ).astype(jnp.bfloat16)
    received = lax.all_to_all(
        send.reshape(experts, capacity, width), "expert", split_axis=0, concat_axis=1, tiled=True
    )
    hidden = jnp.einsum("erd,edf->erf", received, w_up, preferred_element_type=jnp.float32)
    active = jax.nn.gelu(hidden, approximate=False).astype(jnp.bfloat16)
    expert_out = jnp.einsum(
        "erf,efd->erd", active, w_down, preferred_element_type=jnp.float32
    ).astype(jnp.bfloat16)
    returned = lax.all_to_all(expert_out, "expert", split_axis=1, concat_axis=0, tiled=True)
    picked = jnp.einsum(
        "rjs,sd->rjd",
        select,
        returned.reshape(experts * capacity, width),
        preferred_element_type=jnp.float32,
    )
    output = middle + jnp.sum(gates[:, :, None] * picked, axis=1)
    upstream = cotangent.astype(jnp.float32)
    gate_grads = jnp.sum(upstream[:, None, :] * picked, axis=2)
    slot_values = (gates[:, :, None] * upstream[:, None, :]).astype(jnp.bfloat16)
    slot_sends = jnp.einsum(
        "rjs,rjd->sd", select, slot_values, preferred_element_type=jnp.float32
    ).astype(jnp.bfloat16)
    out_grads = lax.all_to_all(
        slot_sends.reshape(experts, capacity, width),
        "expert",
        split_axis=0,
        concat_axis=1,
        tiled=True,
    )
    active_grads = jnp.einsum("erd,efd->erf", out_grads, w_down, preferred_element_type=jnp.float32)
    unused_value, gelu_back = jax.vjp(partial(jax.nn.gelu, approximate=False), hidden)
    hidden_grads = gelu_back(active_grads)[0].astype(jnp.bfloat16)
    row_sends = jnp.einsum(
        "erf,edf->erd", hidden_grads, w_up, preferred_element_type=jnp.float32
    ).astype(jnp.bfloat16)
    row_returns = lax.all_to_all(row_sends, "expert", split_axis=1, concat_axis=0, tiled=True)
    routed_grads = jnp.einsum(
        "rs,sd->rd",
        dispatch_matrix,
        row_returns.reshape(experts * capacity, width),
        preferred_element_type=jnp.float32,
    )
    up_part = jnp.einsum("erd,erf->edf", received, hidden_grads, preferred_element_type=jnp.float32)
    down_part = jnp.einsum("erf,erd->efd", active, out_grads, preferred_element_type=jnp.float32)
    up_grad = lax.psum_scatter(
        up_part.astype(jnp.bfloat16), "context", scatter_dimension=2, tiled=True
    ).astype(jnp.float32)
    down_grad = lax.psum_scatter(
        down_part.astype(jnp.bfloat16), "context", scatter_dimension=1, tiled=True
    ).astype(jnp.float32)
    chosen_grads = gates * (gate_grads - jnp.sum(gates * gate_grads, axis=1, keepdims=True))
    expert_match = (
        routes[:, :, None] == jnp.arange(experts, dtype=jnp.int32)[None, None, :]
    ).astype(jnp.float32)
    logit_grads = jnp.sum(expert_match * chosen_grads[:, :, None], axis=1)
    router_grad = jnp.dot(routed.astype(jnp.float32).T, logit_grads, precision=HIGHEST)
    routed_grads = routed_grads + jnp.dot(
        logit_grads, w_router.astype(jnp.float32).T, precision=HIGHEST
    )
    middle_norm_grads, gain_moe_grad = normalize_back(routed_grads, middle, moe_scale, gain_moe)
    middle_grads = upstream + middle_norm_grads
    branch_grads = middle_grads.astype(jnp.bfloat16)
    proj_grad = jnp.dot(mixed.T, branch_grads, preferred_element_type=jnp.float32)
    mixed_grads = jnp.dot(branch_grads, w_proj.T, preferred_element_type=jnp.float32).astype(
        jnp.bfloat16
    )
    grad_heads = mixed_grads.reshape(rows, HEADS, head_size)
    delta = jnp.einsum("qhd,hqd->hq", grad_heads.astype(jnp.float32), mixed_exact)
    pieces = (
        lax.all_gather(keys, "context", axis=0, tiled=True),
        lax.all_gather(values, "context", axis=0, tiled=True),
    )
    query_acc = jnp.zeros((rows, HEADS, head_size), jnp.float32)
    dist_sum = jnp.zeros((HEADS, 3 * length), jnp.float32)
    key_blocks, size = split_blocks(pieces[0])
    value_blocks, size = split_blocks(pieces[1])
    offsets = size * jnp.arange(key_blocks.shape[0], dtype=jnp.int32)

    def backward_visit(carry, entry):
        query_sum, dist_acc = carry
        key_block, value_block, start = entry
        scores = score_block(query_heads, key_block, first_place, start, dist_table)
        probs = jnp.exp(scores - log_total[:, :, None])
        prob_grads = jnp.einsum(
            "qhd,khd->hqk", grad_heads, value_block, preferred_element_type=jnp.float32
        )
        score_grads = probs * (prob_grads - delta[:, :, None])
        diagonal = diagonal_sums(score_grads)
        where_from = 2 * length + first_place - start - (size - 1)
        span = diagonal.shape[1]
        dist_acc = lax.dynamic_update_slice_in_dim(
            dist_acc,
            lax.dynamic_slice_in_dim(dist_acc, where_from, span, 1) + diagonal,
            where_from,
            1,
        )
        low_scores = score_grads.astype(jnp.bfloat16)
        query_sum = (
            query_sum
            + jnp.einsum("hqk,khd->qhd", low_scores, key_block, preferred_element_type=jnp.float32)
            * scale_factor
        )
        key_part = (
            jnp.einsum("hqk,qhd->khd", low_scores, query_heads, preferred_element_type=jnp.float32)
            * scale_factor
        )
        value_part = jnp.einsum(
            "hqk,qhd->khd",
            probs.astype(jnp.bfloat16),
            grad_heads,
            preferred_element_type=jnp.float32,
        )
        return ((query_sum, dist_acc), (key_part, value_part))

    (query_acc, dist_sum), parts = lax.scan(
        backward_visit, (query_acc, dist_sum), (key_blocks, value_blocks, offsets)
    )
    count = pieces[0].shape[0]
    key_flat = parts[0].reshape(count, width)
    value_flat = parts[1].reshape(count, width)
    key_full = key_flat
    value_full = value_flat
    query_sum, key_full, value_full, dist_sum = (query_acc, key_full, value_full, dist_sum)
    table_grad = jnp.transpose(jnp.dot(dist_sum[:, 2 * length :], bucket_match, precision=HIGHEST))
    key_local, value_local = (
        lax.psum_scatter(
            key_full.astype(jnp.bfloat16), "context", scatter_dimension=0, tiled=True
        ).astype(jnp.float32),
        lax.psum_scatter(
            value_full.astype(jnp.bfloat16), "context", scatter_dimension=0, tiled=True
        ).astype(jnp.float32),
    )
    query_grads = query_sum.reshape(rows, width).astype(jnp.bfloat16)
    key_grads = key_local.astype(jnp.bfloat16)
    value_grads = value_local.astype(jnp.bfloat16)
    query_weight_grad = jnp.dot(normed.T, query_grads, preferred_element_type=jnp.float32)
    key_weight_grad = jnp.dot(normed.T, key_grads, preferred_element_type=jnp.float32)
    value_weight_grad = jnp.dot(normed.T, value_grads, preferred_element_type=jnp.float32)
    normed_grads = jnp.dot(query_grads, w_query.T, preferred_element_type=jnp.float32)
    normed_grads = normed_grads + jnp.dot(key_grads, w_key.T, preferred_element_type=jnp.float32)
    normed_grads = normed_grads + jnp.dot(
        value_grads, w_value.T, preferred_element_type=jnp.float32
    )
    token_norm_grads, gain_attn_grad = normalize_back(
        normed_grads, source, attention_scale, gain_attn
    )
    token_grads = (middle_grads + token_norm_grads).astype(jnp.bfloat16)
    summed = lax.psum(
        (
            gain_attn_grad,
            query_weight_grad,
            key_weight_grad,
            value_weight_grad,
            proj_grad,
            table_grad,
            gain_moe_grad,
            router_grad,
        ),
        ("expert", "context"),
    )
    return (
        output.astype(jnp.bfloat16),
        token_grads,
        summed[0],
        summed[1],
        summed[2],
        summed[3],
        summed[4],
        summed[5],
        summed[6],
        summed[7],
        up_grad,
        down_grad,
    )


def solution(mesh):
    return jax.shard_map(
        shards,
        mesh=mesh,
        in_specs=(
            P(("expert", "context"), None),
            P(),
            P(),
            P(),
            P(),
            P(),
            P(),
            P(),
            P(),
            P("expert", None, None),
            P("expert", None, None),
            P(("expert", "context"), None),
            P(),
            P(("expert", "context"), None),
        ),
        out_specs=(
            P(("expert", "context"), None),
            P(("expert", "context"), None),
            P(),
            P(),
            P(),
            P(),
            P(),
            P(),
            P(),
            P(),
            P("expert", None, "context"),
            P("expert", "context", None),
        ),
        check_vma=False,
    )
```

profile of v0, /device:TPU:0, one launch (start us, length us, event | category | flops | bytes accessed | tf_op | source)
XLA Modules:
  0.0 1490.8 jit_solution(14808412941805423955)
XLA Ops:
  21.8 29.4 %all-gather.5.cloned.1.call-done = bf16[1024,768]{1,0:T(8,128)(2,1)} async-done(((bf16[256,768]{1,0:T(8,128)(2,1)}), bf16[1024,768]{1,0:T(8,128)(2,1)}) %all-gather.5.cloned.1.call-update) | async-done | bytes 1572880 | tf_op jit(solution)/shard_map/all_gather | solution.py:117
  58.2 31.2 %all-gather.3.cloned.1.call-done = bf16[1024,768]{1,0:T(8,128)(2,1)} async-done(((bf16[256,768]{1,0:T(8,128)(2,1)}), bf16[1024,768]{1,0:T(8,128)(2,1)}) %all-gather.3.cloned.1.call-update) | async-done | bytes 1572880 | tf_op jit(solution)/shard_map/all_gather | solution.py:116
  96.3 244.0 %while.41 = (s32[]{:T(128)}, f32[12,256]{1,0:T(8,128)S(1)}, f32[12,256]{1,0:T(8,128)S(1)}, f32[12,256,64]{1,2,0:T(8,128)}, s32[2]{0:T(128)S(1)}, /*index=5*/s32[...) while((s32[]{:T(128)}, f32[12,256]{1,0:T(8,128)S(1)}, ...), condition=%wide.region_4.5_spmd.clone, body=%wide.region_1.4_spmd.clone.sunk | while | flops 416103680 | bytes 180550000 | solution.py:139
  105.1 13.0 copy.223
  118.1 10.2 slice.81
  128.2 20.9 %reshape.436 = f32[12,256,769]{2,1,0:T(8,128)} reshape(f32[12,196864]{1,0:T(8,128)} %slice.81) | data formatting | bytes 18898944 | tf_op jit(solution)/shard_map/while/body/eval_jaxpr/reshape | solution.py:43
  155.3 6.6 copy.224
  161.9 48.4 %rev.35 = f32[12,256,512]{1,2,0:T(8,128)} reverse(f32[12,256,512]{1,2,0:T(8,128)} %copy.224), dimensions={2} | reverse | bytes 12582912 | tf_op jit(solution)/shard_map/while/body/eval_jaxpr/rev | solution.py:44
  226.8 13.0 copy.223
  239.8 10.2 slice.81
  249.9 20.9 %reshape.436 = f32[12,256,769]{2,1,0:T(8,128)} reshape(f32[12,196864]{1,0:T(8,128)} %slice.81) | data formatting | bytes 18898944 | tf_op jit(solution)/shard_map/while/body/eval_jaxpr/reshape | solution.py:43
  283.6 48.4 %rev.35 = f32[12,256,512]{1,2,0:T(8,128)} reverse(f32[12,256,512]{1,2,0:T(8,128)} %copy.224), dimensions={2} | reverse | bytes 12582912 | tf_op jit(solution)/shard_map/while/body/eval_jaxpr/rev | solution.py:44
  360.0 13.1 all-to-all-done
  376.8 36.2 %multiply_convert_fusion = (bf16[1024,3072]{1,0:T(8,128)(2,1)}, f32[1024,3072]{1,0:T(8,128)}, f32[1024,3072]{1,0:T(8,128)}) fusion(bf16[1024,768]{1,0:T(8,128)(2,1)} %bitcast.9, bf16[1,768,3072]{2,1,0:T(8,128)(2,1)} %param.27), kind=kOutput, calls=%fused_computation.55 | convolution fusion | flops 5036310528 | bytes 37748736 | tf_op jit(solution)/shard_map/erd,edf->erf/dot_general | solution.py:166
  413.0 16.2 %add_convert_fusion = bf16[1024,3072]{1,0:T(8,128)(2,1)} fusion(f32[1024,3072]{1,0:T(8,128)} %get-tuple-element.855, f32[1024,3072]{1,0:T(8,128)} %get-tuple-element.862, bf16[1024,768]{1,0:T(8,128)(2,1)S(1)} %bitcast.247, bf16[1,3072,768]{2,1,0:T(8,128)(2,1)} %param.28), kind=kOutput, calls=%fused_computation.54 | convolution fusion | flops 4875878400 | bytes 37748736 | tf_op jit(solution)/shard_map/erd,efd->erf/dot_general | solution.py:192
  429.2 7.5 fusion.79
  441.3 11.2 reduce.5
  458.9 8.5 fusion.76
  471.5 11.3 reduce.6
  498.9 10.8 all-to-all-done.1
  524.7 502.5 %while.42 = (s32[]{:T(128)}, f32[256,12,64]{0,2,1:T(8,128)}, f32[12,3072]{1,0:T(8,128)}, bf16[2,512,12,64]{1,3,2,0:T(8,128)(2,1)}, bf16[2,512,12,64]{1,3,2,0:T(8...) while((s32[]{:T(128)}, f32[256,12,64]{0,2,1:T(8,128)}, ...), condition=%wide.region_19.20_spmd.clone, body=%wide.region_17.19_spmd.clone.sunk | while | flops 1024390400 | bytes 361810112 | solution.py:277
  534.4 13.0 copy.225
  547.4 10.2 slice.83
  557.6 21.0 %reshape.437 = f32[12,256,769]{2,1,0:T(8,128)} reshape(f32[12,196864]{1,0:T(8,128)} %slice.83) | data formatting | bytes 18898944 | tf_op jit(solution)/shard_map/while/body/eval_jaxpr/reshape | solution.py:43
  584.7 6.6 copy.226
  591.3 48.6 %rev.36 = f32[12,256,512]{1,2,0:T(8,128)} reverse(f32[12,256,512]{1,2,0:T(8,128)} %copy.226), dimensions={2} | reverse | bytes 12582912 | tf_op jit(solution)/shard_map/while/body/eval_jaxpr/rev | solution.py:44
  654.5 48.3 %rev.37 = f32[12,256,512]{1,2,0:T(8,128)} reverse(f32[12,256,512]{1,2,0:T(8,128)} %copy-done.1), dimensions={2} | reverse | bytes 12582912 | tf_op jit(solution)/shard_map/while/body/eval_jaxpr/rev | solution.py:67
  702.8 6.6 copy.227
  718.9 16.4 %copy.228 = f32[2,8,256,768]{3,1,2,0:T(8,128)} copy(f32[2,8,256,768]{3,2,1,0:T(8,128)} %bitcast.230) | data formatting | bytes 25165824 | tf_op jit(solution)/shard_map/while
  735.3 10.0 slice.85
  745.3 20.4 %reshape.438 = f32[12,256,767]{2,1,0:T(8,128)} reshape(f32[12,196352]{1,0:T(8,128)} %slice.85) | data formatting | bytes 18849792 | tf_op jit(solution)/shard_map/while/body/eval_jaxpr/reshape | solution.py:69
  782.0 13.0 copy.225
  795.0 10.3 slice.83
  805.2 21.0 %reshape.437 = f32[12,256,769]{2,1,0:T(8,128)} reshape(f32[12,196864]{1,0:T(8,128)} %slice.83) | data formatting | bytes 18898944 | tf_op jit(solution)/shard_map/while/body/eval_jaxpr/reshape | solution.py:43
  832.3 6.6 copy.226
  838.9 48.8 %rev.36 = f32[12,256,512]{1,2,0:T(8,128)} reverse(f32[12,256,512]{1,2,0:T(8,128)} %copy.226), dimensions={2} | reverse | bytes 12582912 | tf_op jit(solution)/shard_map/while/body/eval_jaxpr/rev | solution.py:44
  902.8 48.3 %rev.37 = f32[12,256,512]{1,2,0:T(8,128)} reverse(f32[12,256,512]{1,2,0:T(8,128)} %copy-done.1), dimensions={2} | reverse | bytes 12582912 | tf_op jit(solution)/shard_map/while/body/eval_jaxpr/rev | solution.py:67
  951.1 6.6 copy.227
  967.1 16.4 %copy.228 = f32[2,8,256,768]{3,1,2,0:T(8,128)} copy(f32[2,8,256,768]{3,2,1,0:T(8,128)} %bitcast.230) | data formatting | bytes 25165824 | tf_op jit(solution)/shard_map/while
  983.6 10.0 slice.85
  993.6 20.2 %reshape.438 = f32[12,256,767]{2,1,0:T(8,128)} reshape(f32[12,196352]{1,0:T(8,128)} %slice.85) | data formatting | bytes 18849792 | tf_op jit(solution)/shard_map/while/body/eval_jaxpr/reshape | solution.py:69
  1036.6 9.2 fusion.60
  1045.9 9.8 fusion.61
  1067.4 34.0 %reduce-scatter.5.cloned.1.call-done = bf16[256,768]{0,1:T(8,128)(2,1)} async-done(((bf16[1024,768]{0,1:T(8,128)(2,1)}), bf16[256,768]{0,1:T(8,128)(2,1)}) %reduce-scatter.5.cloned.1.call-update) | async-done | bytes 393232 | tf_op jit(solution)/shard_map/reduce_scatter | solution.py:288
  1112.4 47.0 %all-reduce.2 = (f32[768]{0:T(1024)}, f32[32,12]{0,1:T(8,128)}, f32[768]{0:T(1024)}, f32[768,8]{0,1:T(8,128)}) all-reduce(f32[768]{0:T(1024)S(1)} %get-tuple-element.790, f32[32,12]{0,1:T(8,128)} %fusion.100, f32[768]{0:T(1024)S(1)} %copy-done.55, f32[768,8]{0,1:T(8,128)} %fusion.127), channel_id=1, replica_groups=mesh['expert'=8,'context'=4] {'expert','context'}, use_global_device_ids=true, to_apply=%region_24.25 | all-reduce | flops 8064 | bytes 64512 | tf_op jit(solution)/shard_map/psum | solution.py:310
  1161.0 27.8 %reduce-scatter.9.cloned.1.call-done = bf16[1,768,768]{2,1,0:T(8,128)(2,1)} async-done(((bf16[1,768,3072]{2,1,0:T(8,128)(2,1)}), bf16[1,768,768]{2,1,0:T(8,128)(2,1)}) %reduce-scatter.9.cloned.1.call-update) | async-done | bytes 1179664 | tf_op jit(solution)/shard_map/reduce_scatter | solution.py:207
  1191.7 85.1 %reduce-scatter.11.cloned.1.call-done = bf16[1,768,768]{2,1,0:T(8,128)(2,1)} async-done(((bf16[1,3072,768]{2,1,0:T(8,128)(2,1)}), bf16[1,768,768]{2,1,0:T(8,128)(2,1)}) %reduce-scatter.11.cloned.1.call-update) | async-done | bytes 1179664 | tf_op jit(solution)/shard_map/reduce_scatter | solution.py:210
  1279.6 196.5 %all-reduce.6.cloned.1.call-done = (f32[768,768]{1,0:T(8,128)}, f32[768,768]{1,0:T(8,128)}, f32[768,768]{1,0:T(8,128)}, f32[768,768]{1,0:T(8,128)}) async-done(((f32[768,768]{1,0:T(8,128)}, f32[768,768]{1,0:T(8,128)}, f32[768,768]{1,0:T(8,128)}, f32[768,768]{1,0:T(8,128)}), (f32[768,768]{1,0:T(8,128)}, f32[768,768]{1,0:T(8,128)}, f32[768,768]{1,0:T(8,128)}, ...) | async-done | bytes 9437200 | tf_op jit(solution)/shard_map/psum | solution.py:310
  (333 shorter events, 284.8 us)
Async XLA Ops:
  7.2 13.3 copy-start.42
  7.2 12.1 copy-start.67
  7.3 12.1 copy-start.66
  7.3 43.9 %all-gather.5.cloned.1.call-start = ((), (), s32[]{:S(2)}) async-start(), calls=%async_computation.9 | async-start | bytes 1966080 | tf_op jit(solution)/shard_map/all_gather | solution.py:117
  9.0 44.0 %copy-start.49 = (f32[256]{0:T(256)}, f32[256]{0:T(256)S(1)}, u32[]{:S(2)}) copy-start(f32[256]{0:T(256)S(1)} %add_rsqrt_fusion.1) | copy-start | bytes 3076
  11.3 78.1 %all-gather.3.cloned.1.call-start = ((), (), s32[]{:S(2)}) async-start(), calls=%async_computation.8 | async-start | bytes 1966080 | tf_op jit(solution)/shard_map/all_gather | solution.py:116
  20.5 70.5 %copy-start.60 = (s32[256,2]{0,1:T(2,128)}, s32[256,2]{0,1:T(2,128)S(1)}, u32[]{:S(2)}) copy-start(s32[256,2]{0,1:T(2,128)S(1)} %multiply_add_fusion.1) | copy-start | bytes 6148
  96.3 248.4 %copy-start.51 = (f32[768]{0:T(1024)S(1)}, f32[768]{0:T(1024)}, u32[]{:S(2)}) copy-start(f32[768]{0:T(1024)} %param.25) | copy-start | bytes 9220
  161.9 48.4 %copy-start.2 = (bf16[2,512,12,64]{1,3,2,0:T(8,128)(2,1)S(1)}, bf16[2,512,12,64]{1,3,2,0:T(8,128)(2,1)}, u32[]{:S(2)}) copy-start(bf16[2,512,12,64]{1,3,2,0:T(8,128)(2,1)} %get-tuple-element.1061) | copy-start | bytes 4718596 | tf_op jit(solution)/shard_map/while
  283.6 48.4 %copy-start.2 = (bf16[2,512,12,64]{1,3,2,0:T(8,128)(2,1)S(1)}, bf16[2,512,12,64]{1,3,2,0:T(8,128)(2,1)}, u32[]{:S(2)}) copy-start(bf16[2,512,12,64]{1,3,2,0:T(8,128)(2,1)} %get-tuple-element.1061) | copy-start | bytes 4718596 | tf_op jit(solution)/shard_map/while
  340.3 12.4 copy-start.4
  340.3 12.4 copy-start.27
  340.3 12.5 copy-start.34
  340.3 12.5 copy-start.68
  340.4 11.8 copy-start.43
  340.4 12.1 copy-start.31
  340.4 12.2 copy-start.47
  347.8 25.3 %all-to-all-start = ((bf16[8,128,768]{2,1,0:T(8,128)(2,1)}), bf16[8,128,768]{2,1,0:T(8,128)(2,1)}, u32[]{:S(2)}, u32[]{:S(2)}) async-start(bf16[8,128,768]{2,1,0:T(8,128)(2,1)} %bitcast.8), calls=%async_computation | async-start | bytes 3145728 | tf_op jit(solution)/shard_map/all_to_all | solution.py:163
  357.7 55.2 %copy-start.63 = (f32[256,2]{0,1:T(2,128)}, f32[256,2]{0,1:T(2,128)S(1)}, u32[]{:S(2)}) copy-start(f32[256,2]{0,1:T(2,128)S(1)} %fusion.111) | copy-start | bytes 6148
  373.2 39.8 %all-to-all-start.2 = ((bf16[8,128,768]{2,1,0:T(8,128)(2,1)}), bf16[8,128,768]{2,1,0:T(8,128)(2,1)S(1)}, u32[]{:S(2)}, u32[]{:S(2)}) async-start(bf16[8,128,768]{2,1,0:T(8,128)(2,1)} %bitcast.249), calls=%async_computation.2 | async-start | bytes 3145728 | tf_op jit(solution)/shard_map/all_to_all | solution.py:185
  413.0 16.2 %copy-start.29 = (bf16[8,128,768]{2,1,0:T(8,128)(2,1)}, bf16[8,128,768]{2,1,0:T(8,128)(2,1)S(1)}, u32[]{:S(2)}) copy-start(bf16[8,128,768]{2,1,0:T(8,128)(2,1)S(1)} %all-to-all-done.2) | copy-start | bytes 4718596
  413.0 16.2 %copy-start.65 = (bf16[1,768,3072]{2,1,0:T(8,128)(2,1)S(1)}, bf16[1,768,3072]{2,1,0:T(8,128)(2,1)}, u32[]{:S(2)}) copy-start(bf16[1,768,3072]{2,1,0:T(8,128)(2,1)} %param.27) | copy-start | bytes 14155780
  454.4 30.2 %all-to-all-start.3 = ((bf16[8,2,49152]{2,1,0:T(2,128)(2,1)}), bf16[8,2,49152]{2,1,0:T(2,128)(2,1)}, u32[]{:S(2)}, u32[]{:S(2)}) async-start(bf16[8,2,49152]{2,1,0:T(2,128)(2,1)} %reshape.431), calls=%async_computation.3 | async-start | bytes 3145728 | tf_op jit(solution)/shard_map/all_to_all | solution.py:198
  471.5 17.6 %copy-start.28 = (f32[12,256]{1,0:T(8,128)S(1)}, f32[12,256]{1,0:T(8,128)}, u32[]{:S(2)}) copy-start(f32[12,256]{1,0:T(8,128)} %copy-done.27) | copy-start | bytes 36868
  471.5 17.6 %copy-start.35 = (f32[12,256]{1,0:T(8,128)S(1)}, f32[12,256]{1,0:T(8,128)}, u32[]{:S(2)}) copy-start(f32[12,256]{1,0:T(8,128)} %copy-done.34) | copy-start | bytes 36868
  482.8 12.7 copy-start.26
  484.6 25.1 %all-to-all-start.1 = ((bf16[8,2,49152]{2,1,0:T(2,128)(2,1)}), bf16[8,2,49152]{2,1,0:T(2,128)(2,1)S(1)}, u32[]{:S(2)}, u32[]{:S(2)}) async-start(bf16[8,2,49152]{2,1,0:T(2,128)(2,1)} %reshape.429), calls=%async_computation.1 | async-start | bytes 3145728 | tf_op jit(solution)/shard_map/all_to_all | solution.py:171
  489.0 575.4 %reduce-scatter.7.cloned.1.call-start = ((), (), s32[]{:S(2)}) async-start(), calls=%async_computation.11 | async-start | bytes 1966080 | tf_op jit(solution)/shard_map/reduce_scatter | solution.py:291
  489.1 24.6 %copy-start.62 = (s32[256,2]{0,1:T(2,128)S(1)}, s32[256,2]{0,1:T(2,128)}, u32[]{:S(2)}) copy-start(s32[256,2]{0,1:T(2,128)} %copy-done.60) | copy-start | bytes 6148
  489.1 24.6 %copy-start.64 = (f32[256,2]{0,1:T(2,128)S(1)}, f32[256,2]{0,1:T(2,128)}, u32[]{:S(2)}) copy-start(f32[256,2]{0,1:T(2,128)} %copy-done.63) | copy-start | bytes 6148
  495.5 21.9 %copy-start.46 = (f32[256,2]{0,1:T(2,128)S(1)}, f32[256,2]{0,1:T(2,128)}, u32[]{:S(2)}) copy-start(f32[256,2]{0,1:T(2,128)} %copy-done.45) | copy-start | bytes 6148
  495.5 21.9 %copy-start.54 = (f32[256]{0:T(256)S(1)}, f32[256]{0:T(256)}, u32[]{:S(2)}) copy-start(f32[256]{0:T(256)} %copy-done.53) | copy-start | bytes 3076
  495.5 21.9 %copy-start.57 = (f32[256]{0:T(256)S(1)}, f32[256]{0:T(256)}, u32[]{:S(2)}) copy-start(f32[256]{0:T(256)} %copy-done.56) | copy-start | bytes 3076
  495.5 21.9 %copy-start.44 = (s32[256,2]{0,1:T(2,128)S(1)}, s32[256,2]{0,1:T(2,128)}, u32[]{:S(2)}) copy-start(s32[256,2]{0,1:T(2,128)} %param.29) | copy-start | bytes 6148
  495.5 21.9 %copy-start.48 = (bf16[768,8]{0,1:T(8,128)(2,1)S(1)}, bf16[768,8]{0,1:T(8,128)(2,1)}, u32[]{:S(2)}) copy-start(bf16[768,8]{0,1:T(8,128)(2,1)} %param.26) | copy-start | bytes 36868
  495.5 21.9 %copy-start.52 = (f32[768]{0:T(1024)S(1)}, f32[768]{0:T(1024)}, u32[]{:S(2)}) copy-start(f32[768]{0:T(1024)} %param.25) | copy-start | bytes 9220
  495.5 21.9 %copy-start.59 = (f32[256]{0:T(256)S(1)}, f32[256]{0:T(256)}, u32[]{:S(2)}) copy-start(f32[256]{0:T(256)} %copy-done.58) | copy-start | bytes 3076
  591.3 48.6 %copy-start.3 = (bf16[2,512,12,64]{1,3,2,0:T(8,128)(2,1)S(1)}, bf16[2,512,12,64]{1,3,2,0:T(8,128)(2,1)}, u32[]{:S(2)}) copy-start(bf16[2,512,12,64]{1,3,2,0:T(8,128)(2,1)} %get-tuple-element.1119) | copy-start | bytes 4718596 | tf_op jit(solution)/shard_map/while
  838.9 48.8 %copy-start.3 = (bf16[2,512,12,64]{1,3,2,0:T(8,128)(2,1)S(1)}, bf16[2,512,12,64]{1,3,2,0:T(8,128)(2,1)}, u32[]{:S(2)}) copy-start(bf16[2,512,12,64]{1,3,2,0:T(8,128)(2,1)} %get-tuple-element.1119) | copy-start | bytes 4718596 | tf_op jit(solution)/shard_map/while
  1031.8 69.5 %reduce-scatter.5.cloned.1.call-start = ((), (), s32[]{:S(2)}) async-start(), calls=%async_computation.10 | async-start | bytes 1966080 | tf_op jit(solution)/shard_map/reduce_scatter | solution.py:288
  1036.5 152.3 %reduce-scatter.9.cloned.1.call-start = ((), (), s32[]{:S(2)}) async-start(), calls=%async_computation.12 | async-start | bytes 5898240 | tf_op jit(solution)/shard_map/reduce_scatter | solution.py:207
  1045.8 11.5 copy-start.14
  1045.8 11.5 copy-start.39
  1045.8 11.5 copy-start.50
  1045.8 230.9 %reduce-scatter.11.cloned.1.call-start = ((), (), s32[]{:S(2)}) async-start(), calls=%async_computation.13 | async-start | bytes 5898240 | tf_op jit(solution)/shard_map/reduce_scatter | solution.py:210
  1055.8 420.3 %all-reduce.6.cloned.1.call-start = ((), (), s32[]{:S(2)}) async-start(), calls=%async_computation.14 | async-start | bytes 18874368 | tf_op jit(solution)/shard_map/psum | solution.py:310
  1067.4 38.9 %copy-start.19 = (bf16[256,768]{1,0:T(8,128)(2,1)S(1)}, bf16[256,768]{1,0:T(8,128)(2,1)}, u32[]{:S(2)}) copy-start(bf16[256,768]{1,0:T(8,128)(2,1)} %copy-done.18) | copy-start | bytes 1179652
  1067.4 38.9 %copy-start.41 = (f32[256,8]{0,1:T(8,128)S(1)}, f32[256,8]{0,1:T(8,128)}, u32[]{:S(2)}) copy-start(f32[256,8]{0,1:T(8,128)} %copy-done.40) | copy-start | bytes 24580
  (42 other events, 190.4 us)
Sparse Core Ops, SparseCore 0:
  11.4 39.7 all-gather.4
  53.4 35.9 all-gather.2
  1031.9 32.3 reduce-scatter.6
  1067.1 34.2 reduce-scatter.4
  1103.5 85.2 reduce-scatter.8
  1191.0 85.7 reduce-scatter.10
  1283.5 192.4 all-reduce.5
where the time goes:
time: 1520 us; the launch traced here: 1490 us
  local copies, waits for them, and re-layouts  747 us (49%)
  waiting for transfers between devices  431 us (28%)
  matrix products  169 us (11%)
  other arithmetic  51.6 us (3%)
  blocking collectives  47 us (3%)
  starting transfers between devices  17.3 us (1%)
  between operations  15.4 us (1%)
    psum x1, waiting for transfers between devices, shards(): lax.psum((gain_attn_grad, query_weight_grad, key_weight_grad, value_weigh...  196 us
    rev x4, local copies, waits for them, and re-layouts, bias_window(): return skewed[:, :, :key_count][:, :, ::-1]  194 us
    while x56, local copies, waits for them, and re-layouts  162 us
    rev x2, local copies, waits for them, and re-layouts, diagonal_sums(): turned = jnp.pad(grid[:, :, ::-1], ((0, 0), (0, 0), (0, count)))  96.6 us
    reduce_scatter x1, waiting for transfers between devices, shards(): lax.psum_scatter(down_part.astype(jnp.bfloat16), 'context', scatter_dimen...  85.1 us
    reshape x4, local copies, waits for them, and re-layouts, bias_window(): skewed = tiled.reshape(heads, query_count, span + 1)  83.7 us
    psum x1, blocking collectives, shards(): lax.psum((gain_attn_grad, query_weight_grad, key_weight_grad, value_weigh...  47 us
    slice x4, local copies, waits for them, and re-layouts, bias_window(): tiled = jnp.tile(window, (1, query_count + 1))[:, :query_count * (span + 1)]  40.8 us
  transfers between devices with their start and end apart: 11, of which 9 were waited for; matrix products, arithmetic and copies ran while one was open for 10% of the time, Pallas kernels for 0%

commit v1 on v0

v1 whole, which is shorter than its diff:
```python
from functools import partial

import jax
import jax.numpy as jnp
from jax import lax
from jax.experimental import pallas as pl
from jax.experimental.pallas import tpu as pltpu
from jax.sharding import PartitionSpec as P

HEADS = 12
EPSILON = 1e-06
HIGHEST = lax.Precision.HIGHEST
MASKED = -1000000000.0
F32 = jnp.float32
BF16 = jnp.bfloat16
VMEM_LIMIT = 56 * 1024 * 1024
FF_TILE = 512
SPARE = 8


def dot(left, right, dims=((1,), (0,))):
    return lax.dot_general(left, right, (dims, ((), ())), preferred_element_type=F32)


def normalize(value, gain):
    scale = lax.rsqrt(jnp.mean(value * value, axis=1, keepdims=True) + EPSILON)
    return (value * scale * gain, scale)


def normalize_back(grad, value, scale, gain):
    normal = value * scale
    inner = grad * gain
    gain_grad = jnp.sum(grad * normal, axis=0)
    value_grad = scale * (inner - normal * jnp.mean(inner * normal, axis=1, keepdims=True))
    return (value_grad, gain_grad)


def shift(value, axis, step):
    count = lax.axis_size(axis)
    return lax.ppermute(value, axis, [(i, (i + step) % count) for i in range(count)])


def swap(value, axis, bit):
    count = lax.axis_size(axis)
    return lax.ppermute(value, axis, [(i, i ^ bit) for i in range(count)])


def ring_gather(value, axis):
    count = lax.axis_size(axis)
    here = lax.axis_index(axis)
    size = value.shape[0]
    parts = [(0, value)]
    right = left = value
    for step in range(1, count // 2 + 1):
        right = shift(right, axis, 1)
        parts.append((step, right))
        if step <= (count - 1) // 2:
            left = shift(left, axis, -1)
            parts.append((count - step, left))
    whole = jnp.zeros((count * size,) + value.shape[1:], value.dtype)
    for step, part in parts:
        whole = lax.dynamic_update_slice_in_dim(
            whole, part, lax.rem(here - step + count, count) * size, 0
        )
    return whole


def bit_orders(count):
    bits = [1 << i for i in range(count.bit_length() - 1)]
    return bits[:1] + bits[:0:-1]


def halve_sum(value, axis, bits):
    here = lax.axis_index(axis)
    for bit in bits:
        pair = value.reshape((2, value.shape[0] // 2) + value.shape[1:])
        mine = lax.rem(here // bit, 2)
        kept = lax.dynamic_index_in_dim(pair, mine, 0, keepdims=False)
        sent = lax.dynamic_index_in_dim(pair, 1 - mine, 0, keepdims=False)
        value = (kept.astype(F32) + swap(sent, axis, bit).astype(F32)).astype(value.dtype)
    return value[0]


def double_gather(value, axis, bits):
    here = lax.axis_index(axis)
    value = value[None]
    for bit in bits[::-1]:
        other = swap(value, axis, bit)
        first = lax.rem(here // bit, 2) == 0
        value = jnp.concatenate(
            [jnp.where(first, value, other), jnp.where(first, other, value)], axis=0
        )
    return value


def attend_kernel(tokens, gain, weight, bias, normed, qkv, mixed, exact, log_total, tiles):
    length = tokens.shape[0]
    count, size, tile = mixed.shape

    @pl.when(pl.program_id(0) == 0)
    def _():
        def body(i, carry):
            part = pl.ds(i * tile, tile)
            normal, unused = normalize(tokens[part, :].astype(F32), gain[...])
            normed[part, :] = normal.astype(BF16)
            return carry

        lax.fori_loop(0, count, body, 0)

    weight_all = weight[...].reshape(3 * size, weight.shape[2])
    key_parts = []
    for i in range(count):
        part = dot(weight_all, normed[i * tile : (i + 1) * tile, :], ((1,), (1,)))
        low = part.astype(BF16)
        for j in range(3):
            qkv[j, :, i * tile : (i + 1) * tile] = low[j * size : (j + 1) * size, :]
        key_parts.append(part[size : 2 * size, :].T.astype(BF16))
        wide = jnp.broadcast_to(bias[0, :, i * tile : (i + 2) * tile], (tile, 2 * tile))
        turned = pltpu.roll(wide, tile, 1, stride=1, stride_axis=0)
        tiles[(count - 1 - i) * tile : (count - i) * tile, :] = turned[:, :tile]
    keys = jnp.concatenate(key_parts, axis=0)
    factor = size ** (-0.5)
    for i in range(count):
        cols = slice(i * tile, (i + 1) * tile)
        many = (i + 1) * tile
        scores = dot(keys[:many], qkv[0, :, cols]) * factor + tiles[length - many :, :]
        peak = jnp.max(scores, axis=0, keepdims=True)
        weights = jnp.exp(scores - peak)
        total = jnp.sum(weights, axis=0, keepdims=True)
        result = dot(qkv[2, :, :many], weights.astype(BF16)) * (1.0 / total)
        exact[0, :, cols] = result
        mixed[i, :, :] = result.astype(BF16)
        log_total[0, :, cols] = peak + jnp.log(total)


def fold(grid):
    tile = grid.shape[0]
    value = jnp.concatenate([jnp.zeros_like(grid), grid], axis=1)
    half = tile // 2
    while half >= 8:
        value = value[:half] + pltpu.roll(value[half:], 2 * tile - half, 1)
        half //= 2
    return value


def attend_back_kernel(
    qkv, normed, bias, log_total, exact, grads_in, grads, weight_grads, diagonals,
    tiles, sums, keys_acc, values_acc, query_acc,
):
    count, size, tile = grads_in.shape
    factor = size ** (-0.5)
    queries, values, outs, deltas = [], [], [], []
    keys = []
    for i in range(count):
        cols = slice(i * tile, (i + 1) * tile)
        queries.append(qkv[0, :, cols].astype(F32).T.astype(BF16))
        keys.append(qkv[1, :, cols].astype(F32).T.astype(BF16))
        values.append(qkv[2, :, cols].astype(F32).T.astype(BF16))
        out = grads_in[i].astype(F32)
        outs.append(out.T.astype(BF16))
        deltas.append(jnp.sum(out * exact[0, :, cols], axis=0, keepdims=True))
        wide = jnp.broadcast_to(bias[0, :, i * tile : (i + 2) * tile], (tile, 2 * tile))
        turned = pltpu.roll(wide, tile, 1, stride=1, stride_axis=0)
        tiles[i] = turned[:, :tile]
    for d in range(count):
        for j in range(count - d):
            i = j + d
            cols = slice(i * tile, (i + 1) * tile)
            scores = dot(keys[j], qkv[0, :, cols]) * factor + tiles[d]
            probs = jnp.exp(scores - log_total[0, :, cols])
            prob_grads = dot(values[j], grads_in[i])
            score_grads = probs * (prob_grads - deltas[i])
            low = score_grads.astype(BF16)
            value_part = dot(probs.astype(BF16), outs[i])
            key_part = dot(low, queries[i])
            query_part = dot(qkv[1, :, j * tile : (j + 1) * tile], low)
            if j == 0:
                sums[...] = score_grads
            else:
                sums[...] += score_grads
            if d == 0:
                values_acc[j] = value_part
                keys_acc[j] = key_part
                query_acc[i] = query_part
            else:
                values_acc[j] += value_part
                keys_acc[j] += key_part
                query_acc[i] += query_part
        rows = fold(sums[...])
        line = rows[0:1]
        for r in range(1, 8):
            line = line + pltpu.roll(rows[r : r + 1], 2 * tile - r, 1)
        if d == 0:
            diagonals[0, :, : 2 * tile] = line
        else:
            diagonals[0, :, d * tile : (d + 1) * tile] += line[:, :tile]
            diagonals[0, :, (d + 1) * tile : (d + 2) * tile] = line[:, tile:]
    total = None
    for i in range(count):
        query_part = (query_acc[i] * factor).astype(BF16)
        key_part = (keys_acc[i] * factor).T.astype(BF16)
        value_part = values_acc[i].T.astype(BF16)
        grads[i, 0] = query_part
        grads[i, 1] = key_part
        grads[i, 2] = value_part
        stacked = jnp.concatenate([query_part, key_part, value_part], axis=0)
        part = dot(stacked, normed[i * tile : (i + 1) * tile, :])
        total = part if total is None else total + part
    for j in range(3):
        weight_grads[j] = total[j * size : (j + 1) * size, :].astype(BF16)


def expert_kernel(rows_in, out_grads, up, down, active, hidden_grads, row_grads, gate_sums, acc):
    step = pl.program_id(0)
    hidden = dot(rows_in[...], up[...])
    active_grads = dot(out_grads[...], down[...], ((1,), (1,)))
    below = 0.5 * (1.0 + lax.erf(hidden * (0.5**0.5)))
    density = jnp.exp(-0.5 * hidden * hidden) * 0.3989422804014327
    low_active = (hidden * below).astype(BF16)
    active[...] = low_active
    low_grads = (active_grads * (below + hidden * density)).astype(BF16)
    hidden_grads[...] = low_grads
    part = dot(low_grads, up[...], ((1,), (1,)))
    sums = jnp.sum(low_active.astype(F32) * active_grads, axis=1, keepdims=True)

    @pl.when(step == 0)
    def _():
        acc[...] = part
        gate_sums[...] = sums

    @pl.when(step > 0)
    def _():
        acc[...] += part
        gate_sums[...] += sums

    @pl.when(step == pl.num_programs(0) - 1)
    def _():
        row_grads[...] = acc[...].astype(BF16)


def params():
    return pltpu.CompilerParams(
        dimension_semantics=("arbitrary",), vmem_limit_bytes=VMEM_LIMIT
    )


def attend(tokens, gain, weight, bias, count):
    length, width = tokens.shape
    group = bias.shape[0]
    size = weight.shape[1] // group
    tile = length // count
    return pl.pallas_call(
        attend_kernel,
        grid=(group,),
        in_specs=[
            pl.BlockSpec((length, width), lambda h: (0, 0)),
            pl.BlockSpec((1, width), lambda h: (0, 0)),
            pl.BlockSpec((3, size, width), lambda h: (0, h, 0)),
            pl.BlockSpec((1, 1, length + tile), lambda h: (h, 0, 0)),
        ],
        out_specs=[
            pl.BlockSpec((length, width), lambda h: (0, 0)),
            pl.BlockSpec((3, size, length), lambda h: (0, h, 0)),
            pl.BlockSpec((count, size, tile), lambda h: (0, h, 0)),
            pl.BlockSpec((1, size, length), lambda h: (h, 0, 0)),
            pl.BlockSpec((1, 1, length), lambda h: (h, 0, 0)),
        ],
        out_shape=[
            jax.ShapeDtypeStruct((length, width), BF16),
            jax.ShapeDtypeStruct((3, group * size, length), BF16),
            jax.ShapeDtypeStruct((count, group * size, tile), BF16),
            jax.ShapeDtypeStruct((group, size, length), F32),
            jax.ShapeDtypeStruct((group, 1, length), F32),
        ],
        scratch_shapes=[pltpu.VMEM((length, tile), F32)],
        compiler_params=params(),
        name="attend",
    )(tokens, gain, weight, bias)


def attend_back(qkv, normed, bias, log_total, exact, grads_in):
    length, width = normed.shape
    count, _, tile = grads_in.shape
    group, size, _ = exact.shape
    return pl.pallas_call(
        attend_back_kernel,
        grid=(group,),
        in_specs=[
            pl.BlockSpec((3, size, length), lambda h: (0, h, 0)),
            pl.BlockSpec((length, width), lambda h: (0, 0)),
            pl.BlockSpec((1, 1, length + tile), lambda h: (h, 0, 0)),
            pl.BlockSpec((1, 1, length), lambda h: (h, 0, 0)),
            pl.BlockSpec((1, size, length), lambda h: (h, 0, 0)),
            pl.BlockSpec((count, size, tile), lambda h: (0, h, 0)),
        ],
        out_specs=[
            pl.BlockSpec((count, 3, size, tile), lambda h: (0, 0, h, 0)),
            pl.BlockSpec((3, size, width), lambda h: (0, h, 0)),
            pl.BlockSpec((1, 1, length + tile), lambda h: (h, 0, 0)),
        ],
        out_shape=[
            jax.ShapeDtypeStruct((count, 3, group * size, tile), BF16),
            jax.ShapeDtypeStruct((3, group * size, width), BF16),
            jax.ShapeDtypeStruct((group, 1, length + tile), F32),
        ],
        scratch_shapes=[
            pltpu.VMEM((count, tile, tile), F32),
            pltpu.VMEM((tile, tile), F32),
            pltpu.VMEM((count, tile, size), F32),
            pltpu.VMEM((count, tile, size), F32),
            pltpu.VMEM((count, size, tile), F32),
        ],
        compiler_params=params(),
        name="attend_back",
    )(qkv, normed, bias, log_total, exact, grads_in)


def expert(rows_in, out_grads, up, down):
    rows, width = rows_in.shape
    hidden = up.shape[1]
    return pl.pallas_call(
        expert_kernel,
        grid=(hidden // FF_TILE,),
        in_specs=[
            pl.BlockSpec((rows, width), lambda f: (0, 0)),
            pl.BlockSpec((rows, width), lambda f: (0, 0)),
            pl.BlockSpec((width, FF_TILE), lambda f: (0, f)),
            pl.BlockSpec((FF_TILE, width), lambda f: (f, 0)),
        ],
        out_specs=[
            pl.BlockSpec((rows, FF_TILE), lambda f: (0, f)),
            pl.BlockSpec((rows, FF_TILE), lambda f: (0, f)),
            pl.BlockSpec((rows, width), lambda f: (0, 0)),
            pl.BlockSpec((rows, 1), lambda f: (0, 0)),
        ],
        out_shape=[
            jax.ShapeDtypeStruct((rows, hidden), BF16),
            jax.ShapeDtypeStruct((rows, hidden), BF16),
            jax.ShapeDtypeStruct((rows, width), BF16),
            jax.ShapeDtypeStruct((rows, 1), F32),
        ],
        scratch_shapes=[pltpu.VMEM((rows, width), F32)],
        compiler_params=params(),
        name="expert",
    )(rows_in, out_grads, up, down)


def chosen_softmax(logits, chosen, axis):
    peak = jnp.max(jnp.where(chosen, logits, -jnp.inf), axis=axis, keepdims=True)
    peak = jnp.where(peak > -jnp.inf, peak, 0.0)
    parts = jnp.where(chosen, jnp.exp(jnp.where(chosen, logits, peak) - peak), 0.0)
    total = jnp.sum(parts, axis=axis, keepdims=True)
    return parts / jnp.where(total > 0.0, total, 1.0)


def to_experts(value):
    return lax.all_to_all(value, "expert", split_axis=0, concat_axis=0)


def to_context(value):
    return lax.all_to_all(value, "context", split_axis=0, concat_axis=0)


def shards(
    tokens,
    gain_attn,
    w_query,
    w_key,
    w_value,
    w_proj,
    bias_table,
    gain_moe,
    w_router,
    w_up,
    w_down,
    routes,
    bucket_ids,
    cotangent,
):
    rows, width = tokens.shape
    size = width // HEADS
    experts = w_router.shape[1]
    buckets = bias_table.shape[0]
    picks = routes.shape[1]
    capacity = 2 * rows * picks // experts
    slots = experts * capacity
    count = lax.axis_size("context")
    lanes = lax.axis_size("expert")
    here = lax.axis_index("context")
    own = lax.axis_index("expert")
    length = rows * count
    group = -(-HEADS // count)
    held = group * size
    extra = count * group - HEADS

    sequence = ring_gather(tokens, "context")

    expert_ids = jnp.arange(experts, dtype=jnp.int32)
    chosen = jnp.any(routes[:, :, None] == expert_ids[None, None, :], axis=1)
    member = chosen.astype(BF16)
    order = jnp.arange(rows, dtype=jnp.int32)
    earlier = (order[:, None] > order[None, :]).astype(BF16)
    place = dot(earlier, member).astype(jnp.int32)
    dispatch = (
        (place[:, :, None] == jnp.arange(capacity, dtype=jnp.int32)[None, None, :])
        & chosen[:, :, None]
    ).astype(BF16)
    dispatch = dispatch.reshape(rows, slots)

    upstream_slots = to_experts(
        dot(dispatch, cotangent, ((0,), (0,))).astype(BF16).reshape(experts, capacity, width)
    ).reshape(slots, width)
    choices = dot(member, dispatch, ((0,), (0,))).astype(BF16)
    choices = jnp.transpose(choices.reshape(experts, experts, capacity), (1, 0, 2))
    choices = jnp.transpose(to_experts(choices), (1, 0, 2)) > 0.5

    def head_rows(weight):
        whole = jnp.pad(weight, ((0, 0), (0, extra * size)))
        return lax.dynamic_slice_in_dim(whole, here * held, held, 1).T

    head_weights = jnp.stack([head_rows(w) for w in (w_query, w_key, w_value)])
    bucket_match = (
        bucket_ids[:, None] == jnp.arange(buckets, dtype=jnp.int32)[None, :]
    ).astype(F32)
    per_distance = lax.dot_general(
        jnp.pad(bias_table, ((0, 0), (0, extra))), bucket_match, (((0,), (1,)), ((), ())),
        precision=HIGHEST,
    )
    bias = jnp.pad(
        lax.dynamic_slice_in_dim(per_distance, here * group, group, 0),
        ((0, 0), (rows, 0)),
        constant_values=MASKED,
    )[:, None, :]
    normed, qkv, mixed_parts, exact, log_total = attend(
        sequence, gain_attn[None, :], head_weights, bias, count
    )
    mixed = to_context(mixed_parts).reshape(count * held, rows)[:width]
    source = tokens.astype(F32)
    middle = source + dot(mixed, w_proj, ((0,), (0,)))
    moe_normal, moe_scale = normalize(middle, gain_moe)
    routed = moe_normal.astype(BF16)

    received = to_experts(
        dot(dispatch, routed, ((0,), (0,))).astype(BF16).reshape(experts, capacity, width)
    ).reshape(slots, width)
    slot_logits = dot(w_router, received, ((0,), (1,))).reshape(experts, lanes, capacity)
    slot_gates = chosen_softmax(slot_logits, choices, 0)
    slot_gate = lax.dynamic_index_in_dim(slot_gates, own, 0, keepdims=False).reshape(slots, 1)
    out_grads = (slot_gate * upstream_slots.astype(F32)).astype(BF16)
    active, hidden_grads, row_grads, gate_sums = expert(received, out_grads, w_up[0], w_down[0])
    row_returns = to_experts(row_grads.reshape(experts, capacity, width)).reshape(slots, width)
    gate_returns = to_experts(gate_sums.reshape(experts, capacity))
    expert_out = dot(active, w_down[0]).astype(BF16)
    out_returns = to_experts(expert_out.reshape(experts, capacity, width)).reshape(slots, width)
    up_part = dot(received, hidden_grads, ((0,), (0,))).astype(BF16)
    down_part = dot(active, out_grads, ((0,), (0,))).astype(BF16)
    up_grad = lax.psum_scatter(up_part, "context", scatter_dimension=1, tiled=True).astype(F32)
    down_grad = lax.psum_scatter(down_part, "context", scatter_dimension=0, tiled=True).astype(F32)

    logits = dot(routed, w_router)
    gates = chosen_softmax(logits, chosen, 1)
    spread = dispatch.reshape(rows, experts, capacity).astype(F32)
    gated = (spread * gates[:, :, None]).reshape(rows, slots)
    output = middle + jnp.dot(gated, out_returns.astype(F32), precision=HIGHEST)
    weighted = jnp.sum(spread * gate_returns[None], axis=2)
    logit_grads = jnp.where(
        chosen, weighted - gates * jnp.sum(weighted, axis=1, keepdims=True), 0.0
    )
    router_grad = lax.dot_general(
        logit_grads, routed.astype(F32), (((0,), (0,)), ((), ())), precision=HIGHEST
    )
    routed_grads = dot(dispatch, row_returns) + lax.dot_general(
        logit_grads, w_router.astype(F32), (((1,), (1,)), ((), ())), precision=HIGHEST
    )
    upstream = cotangent.astype(F32)
    middle_norm_grads, gain_moe_grad = normalize_back(routed_grads, middle, moe_scale, gain_moe)
    middle_grads = upstream + middle_norm_grads
    branch_grads = middle_grads.astype(BF16)
    mixed_grads = dot(w_proj, branch_grads, ((1,), (1,))).astype(BF16)
    grads_in = to_context(
        jnp.pad(mixed_grads, ((0, extra * size), (0, 0))).reshape(count, held, rows)
    )
    proj_part = jnp.pad(dot(mixed, branch_grads).astype(BF16), ((0, extra * size), (0, 0)))
    proj_rows = jnp.sum(to_context(proj_part.reshape(count, held, width)).astype(F32), axis=0)

    grads_out, weight_grads, diagonals = attend_back(
        qkv, normed, bias, log_total, exact, grads_in
    )
    table_part = jnp.dot(diagonals[:, 0, rows:], bucket_match, precision=HIGHEST)
    table_line = lax.dynamic_update_slice(
        jnp.zeros((count * group, buckets), F32), table_part, (here * group, 0)
    )[:HEADS].reshape(1, HEADS * buckets)
    table_line = jnp.pad(table_line, ((0, 0), (0, width - HEADS * buckets)))
    small = jnp.concatenate([router_grad, gain_moe_grad[None, :], table_line], axis=0)
    small = jnp.pad(small, ((0, lanes * SPARE - small.shape[0]), (0, 0))).astype(BF16)
    chunk = 4 * held // lanes
    pack = jnp.concatenate(
        [
            jnp.concatenate([weight_grads, proj_rows.astype(BF16)[None]], axis=0).reshape(
                lanes, chunk, width
            ),
            small.reshape(lanes, SPARE, width),
        ],
        axis=1,
    )
    bits = bit_orders(lanes)
    pack = halve_sum(pack, "expert", bits)
    pack = ring_gather(pack[None], "context")
    pack = double_gather(pack, "expert", bits)
    whole = jnp.moveaxis(pack[:, :, :chunk], 1, 0).reshape(count, 4, held, width)

    def rows_of(j):
        return whole[:, j].reshape(count * held, width)[:width].astype(F32)

    grad_query, grad_key, grad_value = rows_of(0).T, rows_of(1).T, rows_of(2).T
    grad_proj = rows_of(3)
    small = jnp.sum(pack[:, :, chunk:].astype(F32), axis=1).reshape(lanes * SPARE, width)
    router_total = small[:experts].T
    gain_moe_total = small[experts]
    table_total = small[experts + 1, : HEADS * buckets].reshape(HEADS, buckets).T
    gain_attn_total = (
        jnp.sum(
            grad_query * w_query.astype(F32)
            + grad_key * w_key.astype(F32)
            + grad_value * w_value.astype(F32),
            axis=1,
        )
        / gain_attn
    )

    arrived = to_context(grads_out)
    normed_grads = 0.0
    for j, weight in enumerate((w_query, w_key, w_value)):
        part = arrived[:, j].reshape(count * held, rows)[:width]
        normed_grads = normed_grads + dot(part, weight, ((0,), (1,)))
    attention_scale = lax.rsqrt(jnp.mean(source * source, axis=1, keepdims=True) + EPSILON)
    token_norm_grads, unused = normalize_back(normed_grads, source, attention_scale, gain_attn)
    token_grads = (middle_grads + token_norm_grads).astype(BF16)
    return (
        output.astype(BF16),
        token_grads,
        gain_attn_total,
        grad_query,
        grad_key,
        grad_value,
        grad_proj,
        table_total,
        gain_moe_total,
        router_total,
        up_grad[None],
        down_grad[None],
    )


def solution(mesh):
    return jax.shard_map(
        shards,
        mesh=mesh,
        in_specs=(
            P(("expert", "context"), None),
            P(),
            P(),
            P(),
            P(),
            P(),
            P(),
            P(),
            P(),
            P("expert", None, None),
            P("expert", None, None),
            P(("expert", "context"), None),
            P(),
            P(("expert", "context"), None),
        ),
        out_specs=(
            P(("expert", "context"), None),
            P(("expert", "context"), None),
            P(),
            P(),
            P(),
            P(),
            P(),
            P(),
            P(),
            P(),
            P("expert", None, "context"),
            P("expert", "context", None),
        ),
        check_vma=False,
    )
```

time: 1520 us -> 476 us (0.31); the launches traced: 1490 us -> 469 us
  local copies, waits for them, and re-layouts: 747 us -> 43.9 us
  waiting for transfers between devices: 431 us -> 213 us
  matrix products: 169 us -> 49.8 us
  Pallas kernels: 0 us -> 47.5 us
  blocking collectives: 47 us -> 7.02 us
  starting transfers between devices: 17.3 us -> 56 us
    rev x6 -> x0, local copies, waits for them, and re-layouts: 291 us -> none  [the longest x4 194 us: bias_window(): return skewed[:, :, :key_count][:, :, ::-1]]
    psum x1 -> x0, waiting for transfers between devices: 196 us -> none  [shards(): lax.psum((gain_attn_grad, query_weight_grad, key_weight_grad, value_weigh...]
    while x56 -> x0, local copies, waits for them, and re-layouts: 162 us -> none
    reduce_scatter x4 -> x2, waiting for transfers between devices: 150 us -> 0.01 us  [the longest x1 0.01 us: shards(): lax.psum_scatter(down_part, 'context', scatter_dimension=0, tiled=True)]
    all_to_all x4 -> x9, waiting for transfers between devices: 23.9 us -> 157 us  [the longest x4 81.9 us: to_context(): return lax.all_to_all(value, 'context', split_axis=0, concat_axis=0)]
    reshape x10 -> x1, local copies, waits for them, and re-layouts: 129 us -> 0.09 us  [shards(): table_line = lax.dynamic_update_slice(jnp.zeros((count * group, buckets),...]
    dot_general x41 -> x21, matrix products: 169 us -> 49.8 us  [the longest x16 42.9 us: dot(): lax.dot_general(left, right, (dims, ((), ())), preferred_element_type=F32)]
    slice x11 -> x5, local copies, waits for them, and re-layouts: 85.6 us -> 4.84 us  [the longest x1 1.41 us: shards(): part = arrived[:, j].reshape(count * held, rows)[:width]]
  transfers between devices with their start and end apart: 11 -> 23, of which waited for: 9 -> 17; matrix products, arithmetic and copies ran while one was open for 10% -> 22% of each run, Pallas kernels for 0% -> 3%
where the time goes in v1:
time: 476 us; the launch traced here: 469 us
  waiting for transfers between devices  213 us (45%)
  starting transfers between devices  56 us (12%)
  matrix products  49.8 us (10%)
  Pallas kernels  47.5 us (10%)
  local copies, waits for them, and re-layouts  43.9 us (9%)
  other arithmetic  36.5 us (8%)
  between operations  15.3 us (3%)
  blocking collectives  7.02 us (1%)
    all_to_all x4, waiting for transfers between devices, to_context(): return lax.all_to_all(value, 'context', split_axis=0, concat_axis=0)  81.9 us
    all_to_all x5, waiting for transfers between devices, to_experts(): return lax.all_to_all(value, 'expert', split_axis=0, concat_axis=0)  74.7 us
    dot_general x16, matrix products, dot(): lax.dot_general(left, right, (dims, ((), ())), preferred_element_type=F32)  42.9 us
    ppermute x6, waiting for transfers between devices, swap(): return lax.ppermute(value, axis, [(i, i ^ bit) for i in range(count)])  36.7 us
    unnamed x114, local copies, waits for them, and re-layouts  24 us
    pallas_call x1, Pallas kernels, expert(): pl.pallas_call(expert_kernel, grid=(hidden // FF_TILE,), in_specs=[pl.Blo...  23.8 us
    all_to_all x5, starting transfers between devices, to_experts(): return lax.all_to_all(value, 'expert', split_axis=0, concat_axis=0)  19.8 us
    ppermute x6, waiting for transfers between devices, shift(): lax.ppermute(value, axis, [(i, (i + step) % count) for i in range(count)])  19.4 us
  transfers between devices with their start and end apart: 23, of which 17 were waited for; matrix products, arithmetic and copies ran while one was open for 22% of the time, Pallas kernels for 3%

profile of v1, /device:TPU:0, one launch (start us, length us, event | category | flops | bytes accessed | tf_op | source)
XLA Modules:
  0.0 468.7 jit_solution(12278806800107698650)
XLA Ops:
  7.2 5.1 %collective-permute-start.1 = (bf16[256,768]{1,0:T(8,128)(2,1)}, bf16[256,768]{1,0:T(8,128)(2,1)}, u32[]{:S(2)}, u32[]{:S(2)}) collective-permute-start(bf16[256,768]{1,0:T(8,128)(2,1)} %param.14), channel_id=1, source_target_pairs={{0,3},{1,0},{2,1},{3,2},{4,7},{5,4},{6,5},{7,6},{8,11},{9,8},{10,9... | collective-permute-start | bytes 1179656 | tf_op jit(solution)/shard_map/ppermute | solution.py:40
  13.9 2.8 copy.69
  18.7 2.4 copy.67
  22.6 7.7 %collective-permute-done = bf16[256,768]{1,0:T(8,128)(2,1)} collective-permute-done((bf16[256,768]{1,0:T(8,128)(2,1)}, bf16[256,768]{1,0:T(8,128)(2,1)}, u32[]{:S(2)}, u32[]{:S(2)}) %collective-permute-start) | collective-permute-done | bytes 393248 | tf_op jit(solution)/shard_map/ppermute | solution.py:40
  33.2 2.1 pad_maximum_fusion.3.weight
  37.3 5.1 %collective-permute-done.2 = bf16[256,768]{1,0:T(8,128)(2,1)} collective-permute-done((bf16[256,768]{1,0:T(8,128)(2,1)}, bf16[256,768]{1,0:T(8,128)(2,1)}, u32[]{:S(2)}, u32[]{:S(2)}) %collective-permute-start.2) | collective-permute-done | bytes 393248 | tf_op jit(solution)/shard_map/ppermute | solution.py:40
  44.6 10.7 %attend.1 = (bf16[1024,768]{1,0:T(8,128)(2,1)}, bf16[3,192,1024]{2,1,0:T(8,128)(2,1)}, bf16[4,192,256]{2,1,0:T(8,128)(2,1)}, f32[3,64,1024]{2,1,0:T(8,128)}, f32[3,1,1024]{2,1,0:T(1,128)}) custom-call(bf16[1024,768]{1,0:T(8,128)(2,1)} %copy-done.9, f32[1,768]{1,0:T(1,128)} %broadcast_in_dim.112.gain, bf16[3,192,768]{2,1,0:T(8,128)(2,1)} %pad_maximum_fusion.3.weight, ...), custom_call_target="tpu_custom_call" | custom-call | tf_op jit(solution)/shard_map/attend/pallas_call | solution.py:252
  55.3 3.5 all-to-all-start
  60.1 8.8 %all-to-all-done = bf16[4,192,256]{2,1,0:T(8,128)(2,1)S(1)} async-done(((bf16[4,192,256]{2,1,0:T(8,128)(2,1)}), bf16[4,192,256]{2,1,0:T(8,128)(2,1)S(1)}, u32[]{:S(2)}, u32[]{:S(2)}) %all-to-all-start) | async-done | bytes 393248 | tf_op jit(solution)/shard_map/all_to_all | solution.py:361
  68.9 3.7 all-to-all-start.2
  75.1 2.2 all-to-all-done.2
  78.0 3.6 all-to-all-start.1
  81.5 2.8 convolution_convert_fusion.3
  84.4 18.1 %all-to-all-done.1 = bf16[8,128,768]{2,1,0:T(8,128)(2,1)S(1)} async-done(((bf16[8,128,768]{2,1,0:T(8,128)(2,1)}), bf16[8,128,768]{2,1,0:T(8,128)(2,1)S(1)}, u32[]{:S(2)}, u32[]{:S(2)}) %all-to-all-start.1) | async-done | bytes 1572896 | tf_op jit(solution)/shard_map/all_to_all | solution.py:357
  102.5 4.4 all-to-all-start.3
  108.6 19.4 %all-to-all-done.3 = bf16[8,128,768]{2,1,0:T(8,128)(2,1)} async-done(((bf16[8,128,768]{2,1,0:T(8,128)(2,1)}), bf16[8,128,768]{2,1,0:T(8,128)(2,1)}, u32[]{:S(2)}, u32[]{:S(2)}) %all-to-all-start.3) | async-done | bytes 1572896 | tf_op jit(solution)/shard_map/all_to_all | solution.py:357
  128.0 2.9 fusion.1.out_grads
  130.9 23.8 %expert.1 = (bf16[1024,3072]{1,0:T(8,128)(2,1)}, bf16[1024,3072]{1,0:T(8,128)(2,1)}, bf16[1024,768]{1,0:T(8,128)(2,1)}, f32[1024,1]{1,0:T(8,128)}) custom-call(bf16[1024,768]{1,0:T(8,128)(2,1)} %bitcast.178, bf16[1024,768]{1,0:T(8,128)(2,1)} %fusion.1.out_grads, bf16[768,3072]{1,0:T(8,128)(2,1)} %bitcast.184, bf16[3072,768]{1,0:T(8,128)(2,1)} %bitcast.185), custom_call_target="tpu_custom_call" | custom-call | tf_op jit(solution)/shard_map/expert/pallas_call | solution.py:321
  154.7 9.8 %convolution_convert_fusion = bf16[3072,768]{1,0:T(8,128)(2,1)} fusion(bf16[1024,3072]{1,0:T(8,128)(2,1)} %get-tuple-element.25, bf16[1024,768]{1,0:T(8,128)(2,1)S(1)} %copy-done.8), kind=kOutput, calls=%fused_computation.2 | convolution fusion | flops 4834197504 | bytes 12582912 | tf_op jit(solution)/shard_map/dot_general | solution.py:22
  165.7 7.0 %all_to_all.54 = f32[8,1,128]{2,1,0:T(1,128)S(1)} all-to-all(f32[8,1,128]{2,1,0:T(1,128)S(1)} %bitcast.201), channel_id=1, replica_groups=mesh['expert'=8,'context'=4] {'expert'}, dimensions={0} | all-to-all | bytes 8192 | tf_op jit(solution)/shard_map/all_to_all | solution.py:357
  172.7 4.4 all-to-all-start.5
  179.0 19.2 %all-to-all-done.5 = bf16[8,128,768]{2,1,0:T(8,128)(2,1)} async-done(((bf16[8,128,768]{2,1,0:T(8,128)(2,1)}), bf16[8,128,768]{2,1,0:T(8,128)(2,1)}, u32[]{:S(2)}, u32[]{:S(2)}) %all-to-all-start.5) | async-done | bytes 1572896 | tf_op jit(solution)/shard_map/all_to_all | solution.py:357
  198.2 2.1 convolution_bitcast_fusion
  200.4 2.0 multiply_reduce_fusion
  205.8 3.5 all-to-all-start.7
  210.8 18.3 %all-to-all-done.7.grads_in = bf16[4,192,256]{2,1,0:T(8,128)(2,1)S(1)} async-done(((bf16[4,192,256]{2,1,0:T(8,128)(2,1)}), bf16[4,192,256]{2,1,0:T(8,128)(2,1)S(1)}, u32[]{:S(2)}, u32[]{:S(2)}) %all-to-all-start.7) | async-done | bytes 393248 | tf_op jit(solution)/shard_map/all_to_all | solution.py:361
  229.9 7.8 %all-to-all-start.9 = ((bf16[4,192,768]{2,1,0:T(8,128)(2,1)}), bf16[4,192,768]{2,1,0:T(8,128)(2,1)S(1)}, u32[]{:S(2)}, u32[]{:S(2)}) async-start(bf16[4,192,768]{2,1,0:T(8,128)(2,1)} %bitcast.35), calls=%async_computation.9 | async-start | bytes 2359296 | tf_op jit(solution)/shard_map/all_to_all | solution.py:361
  238.3 13.0 %attend_back.1 = (bf16[4,3,192,256]{3,2,1,0:T(8,128)(2,1)}, bf16[3,192,768]{2,1,0:T(8,128)(2,1)}, f32[3,1,1280]{2,1,0:T(1,128)}) custom-call(bf16[3,192,1024]{2,1,0:T(8,128)(2,1)} %get-tuple-element.28.qkv, bf16[1024,768]{1,0:T(8,128)(2,1)} %get-tuple-element.29.normed, f32[3,1,1280]{2,1,0:T(1,128)} %broadcast_in_dim.113.bias, ...), custom_call_target="tpu_custom_call" | custom-call | tf_op jit(solution)/shard_map/attend_back/pallas_call | solution.py:285
  252.6 27.7 %all-to-all-done.9 = bf16[4,192,768]{2,1,0:T(8,128)(2,1)S(1)} async-done(((bf16[4,192,768]{2,1,0:T(8,128)(2,1)}), bf16[4,192,768]{2,1,0:T(8,128)(2,1)S(1)}, u32[]{:S(2)}, u32[]{:S(2)}) %all-to-all-start.9) | async-done | bytes 1179680 | tf_op jit(solution)/shard_map/all_to_all | solution.py:361
  282.7 2.4 collective-permute-done.3
  288.8 8.2 %collective-permute-done.4 = bf16[2,104,768]{2,1,0:T(8,128)(2,1)} collective-permute-done((bf16[2,104,768]{2,1,0:T(8,128)(2,1)S(1)}, bf16[2,104,768]{2,1,0:T(8,128)(2,1)}, u32[]{:S(2)}, u32[]{:S(2)}) %collective-permute-start.4) | collective-permute-done | bytes 319520 | tf_op jit(solution)/shard_map/ppermute | solution.py:45
  300.3 4.2 collective-permute-done.5
  307.0 9.6 %convolution_convert_fusion.1 = bf16[768,3072]{1,0:T(8,128)(2,1)} fusion(bf16[1024,768]{1,0:T(8,128)(2,1)S(1)} %bitcast.179, bf16[1024,3072]{1,0:T(8,128)(2,1)} %get-tuple-element.35), kind=kOutput, calls=%fused_computation.3 | convolution fusion | flops 4834197504 | bytes 12582912 | tf_op jit(solution)/shard_map/dot_general | solution.py:22
  316.6 3.9 collective-permute-start.7
  321.1 2.7 collective-permute-done.7
  324.5 3.8 collective-permute-done.8
  330.0 9.4 %convolution_convert_fusion.2 = bf16[1024,768]{1,0:T(8,128)(2,1)} fusion(bf16[1024,3072]{1,0:T(8,128)(2,1)} %get-tuple-element.25, bf16[1,3072,768]{2,1,0:T(8,128)(2,1)} %param.24), kind=kOutput, calls=%fused_computation.16 | convolution fusion | flops 4832624640 | bytes 12582912 | tf_op jit(solution)/shard_map/dot_general | solution.py:22
  339.4 3.6 all-to-all-start.4
  348.3 15.8 %all-to-all-done.4 = bf16[8,128,768]{2,1,0:T(8,128)(2,1)S(1)} async-done(((bf16[8,128,768]{2,1,0:T(8,128)(2,1)}), bf16[8,128,768]{2,1,0:T(8,128)(2,1)S(1)}, u32[]{:S(2)}, u32[]{:S(2)}) %all-to-all-start.4) | async-done | bytes 1572896 | tf_op jit(solution)/shard_map/all_to_all | solution.py:357
  364.1 4.5 all-to-all-start.8
  368.6 21.9 %collective-permute-done.10 = bf16[2,4,104,768]{3,2,0,1:T(8,128)(2,1)} collective-permute-done((bf16[2,4,104,768]{3,2,0,1:T(8,128)(2,1)}, bf16[2,4,104,768]{3,2,0,1:T(8,128)(2,1)}, u32[]{:S(2)}, u32[]{:S(2)}) %collective-permute-start.10) | collective-permute-done | bytes 1277984 | tf_op jit(solution)/shard_map/ppermute | solution.py:45
  394.4 3.7 fusion.5
  398.1 27.1 %all-to-all-done.8 = bf16[4,3,192,256]{3,2,1,0:T(8,128)(2,1)} async-done(((bf16[4,3,192,256]{3,2,1,0:T(8,128)(2,1)}), bf16[4,3,192,256]{3,2,1,0:T(8,128)(2,1)}, u32[]{:S(2)}, u32[]{:S(2)}) %all-to-all-start.8) | async-done | bytes 1179680 | tf_op jit(solution)/shard_map/all_to_all | solution.py:361
  431.4 2.1 broadcast_select_fusion
  441.3 3.0 copy.82
  446.0 3.0 copy.81
  455.6 2.9 bitcast_convert_fusion
  458.5 2.8 bitcast_convert_fusion.1
  (214 shorter events, 74.7 us)
Async XLA Ops:
  7.2 65.4 %copy-start = (bf16[768,768]{1,0:T(8,128)(2,1)S(1)}, bf16[768,768]{1,0:T(8,128)(2,1)}, u32[]{:S(2)}) copy-start(bf16[768,768]{1,0:T(8,128)(2,1)} %param.19) | copy-start | bytes 3538948
  7.2 29.1 %collective-permute-start.1 = (bf16[256,768]{1,0:T(8,128)(2,1)}, bf16[256,768]{1,0:T(8,128)(2,1)}, u32[]{:S(2)}, u32[]{:S(2)}) collective-permute-start(bf16[256,768]{1,0:T(8,128)(2,1)} %param.14), channel_id=1, source_target_pairs={{0,3},{1,0},{2,1},{3,2},{4,7},{5,4},{6,5},{7,6},{8,11},{9,8},{10,9... | collective-permute-start | bytes 1179656 | tf_op jit(solution)/shard_map/ppermute | solution.py:40
  12.3 18.0 %collective-permute-start = (bf16[256,768]{1,0:T(8,128)(2,1)}, bf16[256,768]{1,0:T(8,128)(2,1)}, u32[]{:S(2)}, u32[]{:S(2)}) collective-permute-start(bf16[256,768]{1,0:T(8,128)(2,1)} %param.14), channel_id=1, source_target_pairs={{0,1},{1,2},{2,3},{3,0},{4,5},{5,6},{6,7},{7,4},{8,9},{9,10},{10,1... | collective-permute-start | bytes 1179656 | tf_op jit(solution)/shard_map/ppermute | solution.py:40
  13.9 2.8 copy-start.12
  18.7 2.5 copy-start.51
  18.7 13.2 %copy-start.40 = (f32[768]{0:T(1024)S(1)}, f32[768]{0:T(1024)}, u32[]{:S(2)}) copy-start(f32[768]{0:T(1024)} %param.15) | copy-start | bytes 9220
  30.3 12.1 %collective-permute-start.2 = (bf16[256,768]{1,0:T(8,128)(2,1)}, bf16[256,768]{1,0:T(8,128)(2,1)}, u32[]{:S(2)}, u32[]{:S(2)}) collective-permute-start(bf16[256,768]{1,0:T(8,128)(2,1)} %collective-permute-done), channel_id=1, source_target_pairs={{0,1},{1,2},{2,3},{3,0},{4,5},{5,6},{6,7},{7,4},{8,9},{9,10},{10,1... | collective-permute-start | bytes 1179656 | tf_op jit(solution)/shard_map/ppermute | solution.py:40
  44.6 14.2 %copy-start.50 = (s32[256,2]{0,1:T(2,128)S(1)}, s32[256,2]{0,1:T(2,128)}, u32[]{:S(2)}) copy-start(s32[256,2]{0,1:T(2,128)} %param.25) | copy-start | bytes 6148
  55.3 13.6 %all-to-all-start = ((bf16[4,192,256]{2,1,0:T(8,128)(2,1)}), bf16[4,192,256]{2,1,0:T(8,128)(2,1)S(1)}, u32[]{:S(2)}, u32[]{:S(2)}) async-start(bf16[4,192,256]{2,1,0:T(8,128)(2,1)} %get-tuple-element.24), calls=%async_computation | async-start | bytes 786432 | tf_op jit(solution)/shard_map/all_to_all | solution.py:361
  58.9 9.9 %copy-start.42 = (s32[256,8]{0,1:T(8,128)}, s32[256,8]{0,1:T(8,128)S(1)}, u32[]{:S(2)}) copy-start(s32[256,8]{0,1:T(8,128)S(1)} %convolution_convert_fusion.9) | copy-start | bytes 24580
  59.2 14.1 %copy-start.22 = (pred[256,1024]{0,1:T(32,128)(4,1)}, pred[256,1024]{0,1:T(32,128)(4,1)S(1)}, u32[]{:S(2)}) copy-start(pred[256,1024]{0,1:T(32,128)(4,1)S(1)} %fusion.13) | copy-start | bytes 786436
  59.2 14.0 %copy-start.38 = (f32[768]{0:T(1024)S(1)}, f32[768]{0:T(1024)}, u32[]{:S(2)}) copy-start(f32[768]{0:T(1024)} %param.21) | copy-start | bytes 9220
  68.9 4.5 copy-start.23
  68.9 8.5 %all-to-all-start.2 = ((bf16[8,8,128]{2,1,0:T(8,128)(2,1)}), bf16[8,8,128]{2,1,0:T(8,128)(2,1)S(1)}, u32[]{:S(2)}, u32[]{:S(2)}) async-start(bf16[8,8,128]{2,1,0:T(8,128)(2,1)} %fusion.9), calls=%async_computation.2 | async-start | bytes 32768 | tf_op jit(solution)/shard_map/all_to_all | solution.py:357
  73.4 4.0 copy-start.10
  78.0 24.5 %all-to-all-start.1 = ((bf16[8,128,768]{2,1,0:T(8,128)(2,1)}), bf16[8,128,768]{2,1,0:T(8,128)(2,1)S(1)}, u32[]{:S(2)}, u32[]{:S(2)}) async-start(bf16[8,128,768]{2,1,0:T(8,128)(2,1)} %bitcast.183), calls=%async_computation.1 | async-start | bytes 3145728 | tf_op jit(solution)/shard_map/all_to_all | solution.py:357
  102.5 4.7 copy-start.2
  102.5 4.7 copy-start.33
  102.5 25.5 %all-to-all-start.3 = ((bf16[8,128,768]{2,1,0:T(8,128)(2,1)}), bf16[8,128,768]{2,1,0:T(8,128)(2,1)}, u32[]{:S(2)}, u32[]{:S(2)}) async-start(bf16[8,128,768]{2,1,0:T(8,128)(2,1)} %bitcast.182), calls=%async_computation.3 | async-start | bytes 3145728 | tf_op jit(solution)/shard_map/all_to_all | solution.py:357
  106.9 348.6 %reduce-scatter.5.cloned.1.call-start = ((), (), s32[]{:S(2)}) async-start(), calls=%async_computation.13 | async-start | bytes 5898240 | tf_op jit(solution)/shard_map/reduce_scatter | solution.py:458
  130.9 23.8 %copy-start.8 = (bf16[1024,768]{1,0:T(8,128)(2,1)S(1)}, bf16[1024,768]{1,0:T(8,128)(2,1)}, u32[]{:S(2)}) copy-start(bf16[1024,768]{1,0:T(8,128)(2,1)} %fusion.1.out_grads) | copy-start | bytes 4718596
  172.7 4.4 copy-start.11
  172.7 5.4 %copy-start.43 = (s32[256,8]{0,1:T(8,128)S(1)}, s32[256,8]{0,1:T(8,128)}, u32[]{:S(2)}) copy-start(s32[256,8]{0,1:T(8,128)} %copy-done.42) | copy-start | bytes 24580
  172.7 25.5 %all-to-all-start.5 = ((bf16[8,128,768]{2,1,0:T(8,128)(2,1)}), bf16[8,128,768]{2,1,0:T(8,128)(2,1)}, u32[]{:S(2)}, u32[]{:S(2)}) async-start(bf16[8,128,768]{2,1,0:T(8,128)(2,1)} %bitcast.192), calls=%async_computation.5 | async-start | bytes 3145728 | tf_op jit(solution)/shard_map/all_to_all | solution.py:357
  202.7 6.6 %copy-start.24 = (bf16[4,192,256]{2,1,0:T(8,128)(2,1)S(1)}, bf16[4,192,256]{2,1,0:T(8,128)(2,1)}, u32[]{:S(2)}) copy-start(bf16[4,192,256]{2,1,0:T(8,128)(2,1)} %copy-done.23) | copy-start | bytes 1179652
  205.8 23.3 %all-to-all-start.7 = ((bf16[4,192,256]{2,1,0:T(8,128)(2,1)}), bf16[4,192,256]{2,1,0:T(8,128)(2,1)S(1)}, u32[]{:S(2)}, u32[]{:S(2)}) async-start(bf16[4,192,256]{2,1,0:T(8,128)(2,1)} %bitcast.31), calls=%async_computation.7 | async-start | bytes 786432 | tf_op jit(solution)/shard_map/all_to_all | solution.py:361
  210.8 27.1 %copy-start.35 = (f32[256,8]{0,1:T(8,128)S(1)}, f32[256,8]{0,1:T(8,128)}, u32[]{:S(2)}) copy-start(f32[256,8]{0,1:T(8,128)} %get-tuple-element.75) | copy-start | bytes 24580
  210.8 27.1 %copy-start.37 = (f32[256,8]{0,1:T(8,128)S(1)}, f32[256,8]{0,1:T(8,128)}, u32[]{:S(2)}) copy-start(f32[256,8]{0,1:T(8,128)} %fusion.44) | copy-start | bytes 24580
  210.8 27.1 %copy-start.48 = (f32[256]{0:T(256)S(1)}, f32[256]{0:T(256)}, u32[]{:S(2)}) copy-start(f32[256]{0:T(256)} %get-tuple-element.74) | copy-start | bytes 3076
  210.8 27.4 %copy-start.49 = (bf16[768]{0:T(1024)(128)(2,1)S(1)}, bf16[768]{0:T(1024)(128)(2,1)}, u32[]{:S(2)}) copy-start(bf16[768]{0:T(1024)(128)(2,1)} %get-tuple-element.72) | copy-start | bytes 4612
  229.9 50.4 %all-to-all-start.9 = ((bf16[4,192,768]{2,1,0:T(8,128)(2,1)}), bf16[4,192,768]{2,1,0:T(8,128)(2,1)S(1)}, u32[]{:S(2)}, u32[]{:S(2)}) async-start(bf16[4,192,768]{2,1,0:T(8,128)(2,1)} %bitcast.35), calls=%async_computation.9 | async-start | bytes 2359296 | tf_op jit(solution)/shard_map/all_to_all | solution.py:361
  237.7 220.8 %reduce-scatter.3.cloned.1.call-start = ((), (), s32[]{:S(2)}) async-start(), calls=%async_computation.12 | async-start | bytes 5898240 | tf_op jit(solution)/shard_map/reduce_scatter | solution.py:457
  238.2 13.8 %copy-start.53 = (s32[1024]{0:T(1024)S(1)}, s32[1024]{0:T(1024)}, u32[]{:S(2)}) copy-start(s32[1024]{0:T(1024)} %param.26) | copy-start | bytes 12292
  282.7 2.4 collective-permute-start.3
  287.2 19.8 %copy-start.3 = (bf16[8,128,768]{2,1,0:T(8,128)(2,1)S(1)}, bf16[8,128,768]{2,1,0:T(8,128)(2,1)}, u32[]{:S(2)}) copy-start(bf16[8,128,768]{2,1,0:T(8,128)(2,1)} %copy-done.2) | copy-start | bytes 4718596
  287.2 9.7 %collective-permute-start.4 = (bf16[2,104,768]{2,1,0:T(8,128)(2,1)S(1)}, bf16[2,104,768]{2,1,0:T(8,128)(2,1)}, u32[]{:S(2)}, u32[]{:S(2)}) collective-permute-start(bf16[2,104,768]{2,1,0:T(8,128)(2,1)S(1)} %dynamic-slice_bitcast_fusion), channel_id=1, source_target_pairs={{0,16},{4,20},{8,24},{12,28},{16,0},{20,4},{24,8},{28,12},{1,17},{... | collective-permute-start | bytes 958472 | tf_op jit(solution)/shard_map/ppermute | solution.py:45
  298.8 5.6 %collective-permute-start.5 = (bf16[1,104,768]{2,1,0:T(8,128)(2,1)}, bf16[1,104,768]{2,1,0:T(8,128)(2,1)}, u32[]{:S(2)}, u32[]{:S(2)}) collective-permute-start(bf16[1,104,768]{2,1,0:T(8,128)(2,1)} %constant_dynamic-slice_fusion), channel_id=1, source_target_pairs={{0,8},{4,12},{8,0},{12,4},{16,24},{20,28},{24,16},{28,20},{1,9},{5... | collective-permute-start | bytes 479240 | tf_op jit(solution)/shard_map/ppermute | solution.py:45
  307.0 13.5 %collective-permute-start.6 = (bf16[1,104,768]{2,1,0:T(8,128)(2,1)}, bf16[1,104,768]{2,1,0:T(8,128)(2,1)S(1)}, u32[]{:S(2)}, u32[]{:S(2)}) collective-permute-start(bf16[1,104,768]{2,1,0:T(8,128)(2,1)} %get-tuple-element.77), channel_id=1, source_target_pairs={{0,1},{1,2},{2,3},{3,0},{4,5},{5,6},{6,7},{7,4},{8,9},{9,10},{10,1... | collective-permute-start | bytes 479240 | tf_op jit(solution)/shard_map/ppermute | solution.py:40
  316.6 7.3 %collective-permute-start.7 = (bf16[1,104,768]{2,1,0:T(8,128)(2,1)}, bf16[1,104,768]{2,1,0:T(8,128)(2,1)S(1)}, u32[]{:S(2)}, u32[]{:S(2)}) collective-permute-start(bf16[1,104,768]{2,1,0:T(8,128)(2,1)} %get-tuple-element.77), channel_id=1, source_target_pairs={{0,3},{1,0},{2,1},{3,2},{4,7},{5,4},{6,5},{7,6},{8,11},{9,8},{10,9... | collective-permute-start | bytes 479240 | tf_op jit(solution)/shard_map/ppermute | solution.py:40
  320.5 7.9 %collective-permute-start.8 = (bf16[1,104,768]{2,1,0:T(8,128)(2,1)S(1)}, bf16[1,104,768]{2,1,0:T(8,128)(2,1)S(1)}, u32[]{:S(2)}, u32[]{:S(2)}) collective-permute-start(bf16[1,104,768]{2,1,0:T(8,128)(2,1)S(1)} %collective-permute-done.6), channel_id=1, source_target_pairs={{0,1},{1,2},{2,3},{3,0},{4,5},{5,6},{6,7},{7,4},{8,9},{9,10},{10,1... | collective-permute-start | bytes 479240 | tf_op jit(solution)/shard_map/ppermute | solution.py:40
  329.0 14.0 %collective-permute-start.9 = (bf16[1,4,104,768]{3,2,0,1:T(8,128)(2,1)}, bf16[1,4,104,768]{3,2,0,1:T(8,128)(2,1)}, u32[]{:S(2)}, u32[]{:S(2)}) collective-permute-start(bf16[1,4,104,768]{3,2,0,1:T(8,128)(2,1)} %bitcast_dynamic-update-slice_fusion.3), channel_id=1, source_target_pairs={{0,8},{4,12},{8,0},{12,4},{16,24},{20,28},{24,16},{28,20},{1,9},{5... | collective-permute-start | bytes 1916936 | tf_op jit(solution)/shard_map/ppermute | solution.py:45
  339.4 24.7 %all-to-all-start.4 = ((bf16[8,128,768]{2,1,0:T(8,128)(2,1)}), bf16[8,128,768]{2,1,0:T(8,128)(2,1)S(1)}, u32[]{:S(2)}, u32[]{:S(2)}) async-start(bf16[8,128,768]{2,1,0:T(8,128)(2,1)} %bitcast.193), calls=%async_computation.4 | async-start | bytes 3145728 | tf_op jit(solution)/shard_map/all_to_all | solution.py:357
  346.4 44.1 %collective-permute-start.10 = (bf16[2,4,104,768]{3,2,0,1:T(8,128)(2,1)}, bf16[2,4,104,768]{3,2,0,1:T(8,128)(2,1)}, u32[]{:S(2)}, u32[]{:S(2)}) collective-permute-start(bf16[2,4,104,768]{3,2,0,1:T(8,128)(2,1)} %pad_maximum_fusion.1), channel_id=1, source_target_pairs={{0,16},{4,20},{8,24},{12,28},{16,0},{20,4},{24,8},{28,12},{1,17},{... | collective-permute-start | bytes 3833864 | tf_op jit(solution)/shard_map/ppermute | solution.py:45
  364.1 4.5 copy-start.26
  364.1 61.2 %all-to-all-start.8 = ((bf16[4,3,192,256]{3,2,1,0:T(8,128)(2,1)}), bf16[4,3,192,256]{3,2,1,0:T(8,128)(2,1)}, u32[]{:S(2)}, u32[]{:S(2)}) async-start(bf16[4,3,192,256]{3,2,1,0:T(8,128)(2,1)} %get-tuple-element.32), calls=%async_computation.8 | async-start | bytes 2359296 | tf_op jit(solution)/shard_map/all_to_all | solution.py:361
  394.2 36.7 %collective-permute-start.11 = (bf16[4,4,104,768]{3,2,0,1:T(8,128)(2,1)}, bf16[4,4,104,768]{3,2,0,1:T(8,128)(2,1)}, u32[]{:S(2)}, u32[]{:S(2)}) collective-permute-start(bf16[4,4,104,768]{3,2,0,1:T(8,128)(2,1)} %pad_maximum_fusion), channel_id=1, source_target_pairs={{0,4},{4,0},{8,12},{12,8},{16,20},{20,16},{24,28},{28,24},{1,5},{5... | collective-permute-start | bytes 7667720 | tf_op jit(solution)/shard_map/ppermute | solution.py:45
  449.3 4.7 copy-start.18
  455.6 5.8 %copy-start.1 = (bf16[768,768]{1,0:T(8,128)(2,1)S(1)}, bf16[768,768]{1,0:T(8,128)(2,1)}, u32[]{:S(2)}) copy-start(bf16[768,768]{1,0:T(8,128)(2,1)} %param.19) | copy-start | bytes 3538948
  (29 other events, 46.9 us)
Sparse Core Ops, SparseCore 0:
  164.6 101.4 reduce-scatter.4
  316.7 105.3 reduce-scatter.2
